TPU v7x, 32 devices: a whole 2x2x4 slice. The times are simulated.
32 devices in a mesh: seq: 8 (over z, x), tp: 4 (over y, core).
Axes of the slice: x: 2, y: 2, z: 4, core: 2. Of those that a mesh axis runs over, the one named last changes fastest.
Arguments:
- layer_input: bfloat16 [2, 4096, 768], P(None, 'seq'), may hold values from -8 to 8
- out_grad: bfloat16 [2, 4096, 768], P(None, 'seq'), may hold values from -6 to 6
- norm1_gain: float32 [768], replicated, may hold values from 0.5 to 1.5
- norm1_shift: float32 [768], replicated, may hold values from -1 to 1
- w_qkv: bfloat16 [768, 3, 768], P(None, None, 'tp'), may hold values from -0.21875 to 0.21875
- w_out: bfloat16 [768, 768], P(None, 'tp'), may hold values from -0.875 to 0.875
- norm2_gain: float32 [768], replicated, may hold values from 0.5 to 1.5
- norm2_shift: float32 [768], replicated, may hold values from -1 to 1
- w_up: bfloat16 [768, 3072], P(None, 'tp'), may hold values from -0.21875 to 0.21875
- w_down: bfloat16 [768, 3072], P(None, 'tp'), may hold values from -0.21875 to 0.21875
- key_keep: int32 [2, 4096], replicated, may hold values from 0 to 1, as said below
- rand_blocks: int32 [2, 64, 3], replicated, may hold values from 0 to 63, as said below
Outputs:
- layer_output: float32 [2, 4096, 768], P(None, ('seq', 'tp'))
- input_grad: float32 [2, 4096, 768], P(None, ('seq', 'tp'))
- grad_w_qkv: float32 [768, 3, 768], P('seq', None, 'tp')
- grad_w_out: float32 [768, 768], P('seq', 'tp')
- grad_w_up: float32 [768, 3072], P('seq', 'tp')
- grad_w_down: float32 [768, 3072], P('seq', 'tp')
- grad_norm1_gain: float32 [768], P('seq')
- grad_norm1_shift: float32 [768], P('seq')
- grad_norm2_gain: float32 [768], P('seq')
- grad_norm2_shift: float32 [768], P('seq')
Inputs may be any that keep to these rules, and one draw needn't show every extreme that they name: `key_keep`: in every block of 64 positions the kept positions come first, 16 or more of them. `rand_blocks`: entry [m, b, j] names a key block of sequence m. Over all 2 sequences, the random blocks of the query blocks held by one index of seq lie on any one index at most 6 times, and exactly 6 times on some index.
All inputs are finite; a program needn't handle non-finite values.
Results may differ from a plain program's by a relative error of at most 0.012.
Values may be sent and summed in bfloat16 or wider, within the bound.
No kernel may reach another device: no remote copies, remote signals or barrier semaphores. Data moves between devices by JAX's collectives and lax.ppermute only.
A program may use at most 384 MiB of HBM per device.

v0:
```python
from functools import partial
import math

import jax
import jax.numpy as jnp
from jax import lax
from jax.sharding import PartitionSpec as P

HEAD_DIM = 64
BLOCK = 64
RANDS = 3


EPS = 1e-06
HIGH = lax.Precision.HIGHEST


def with_halo(block, sides, width):
    for axis, dim in sides:
        count = lax.axis_size(axis)
        forward = [(i, i + 1) for i in range(count - 1)]
        backward = [(target, source) for source, target in forward]
        low = lax.ppermute(
            lax.slice_in_dim(block, block.shape[dim] - width, None, axis=dim), axis, forward
        )
        high = lax.ppermute(lax.slice_in_dim(block, 0, width, axis=dim), axis, backward)
        block = jnp.concatenate([low, block, high], axis=dim)
    return block


def spread(block, axis, source):
    block = jnp.where(lax.axis_index(axis) == source, block, jnp.zeros_like(block))
    return lax.psum(block, axis)


def combined_all(array, axis, join):
    gathered = jax.tree.map(
        lambda a, kind: lax.all_gather(a.astype(kind), axis),
        array,
        (jnp.bfloat16, jnp.bfloat16, jnp.bfloat16),
    )

    def take(source):
        return jax.tree.map(
            lambda a, own: lax.dynamic_index_in_dim(a, source, 0, False).astype(own.dtype),
            gathered,
            array,
        )

    return lax.fori_loop(
        1, lax.axis_size(axis), lambda source, state: join(state, take(source)), take(0)
    )


def layer_norm(hidden, gain, shift):
    center = hidden - jnp.mean(hidden, -1, keepdims=True)
    inverse = lax.rsqrt(jnp.mean(center * center, -1, keepdims=True) + EPS)
    normed = center * inverse
    return (normed * gain + shift, normed, inverse)


def norm_back(grad_rows, normed, inverse, gain):
    scaled = grad_rows * gain
    inner = (
        scaled
        - jnp.mean(scaled, -1, keepdims=True)
        - normed * jnp.mean(scaled * normed, -1, keepdims=True)
    )
    return (
        inner * inverse,
        jnp.sum(grad_rows * normed, axis=(0, 1)),
        jnp.sum(grad_rows, axis=(0, 1)),
    )


def join_rows(former, latter):
    joint_top = jnp.maximum(former[0], latter[0])
    former_scale = jnp.exp(former[0] - joint_top)
    latter_scale = jnp.exp(latter[0] - joint_top)
    return (
        joint_top,
        former[1] * former_scale + latter[1] * latter_scale,
        former[2] * former_scale[..., None] + latter[2] * latter_scale[..., None],
    )


def per_device(
    layer_input,
    out_grad,
    norm1_gain,
    norm1_shift,
    w_qkv,
    w_out,
    norm2_gain,
    norm2_shift,
    w_up,
    w_down,
    key_keep,
    rand_blocks,
):
    batches, tokens_dev, width = layer_input.shape
    local_width = w_qkv.shape[2]
    heads_here = local_width // HEAD_DIM
    devices = lax.axis_size("seq")
    myself = lax.axis_index("seq")
    tp_count = lax.axis_size("tp")
    tp_place = lax.axis_index("tp")
    share_rows = tokens_dev // tp_count
    blocks_dev = tokens_dev // BLOCK
    blocks_all = blocks_dev * devices
    lead_len = 2 * BLOCK
    ref_count = batches * blocks_dev * RANDS
    slots_per = max(1, -(-ref_count // devices))
    inv_root = 1.0 / math.sqrt(HEAD_DIM)
    head_shape = (batches, tokens_dev, heads_here, HEAD_DIM)
    lead_shape = (batches, lead_len, heads_here, HEAD_DIM)
    pad_rows = tokens_dev - BLOCK
    row_ids = jnp.arange(tokens_dev, dtype=jnp.int32)
    first_rows = (myself == 0) & (row_ids < BLOCK)
    last_rows = (myself == devices - 1) & (row_ids >= pad_rows)
    is_lead = first_rows | last_rows

    def own_share(value):
        return lax.dynamic_slice_in_dim(value, tp_place * share_rows, share_rows, 1)

    def head_total(value):
        return lax.psum(value, "tp")

    def place(pair):
        rest = ((0, 0),) * (pair.ndim - 2)
        mask_shape = (1, tokens_dev) + (1,) * (pair.ndim - 2)
        head_part = jnp.pad(pair[:, :BLOCK], ((0, 0), (0, pad_rows)) + rest)
        tail_part = jnp.pad(pair[:, BLOCK:], ((0, 0), (pad_rows, 0)) + rest)
        return jnp.where(
            first_rows.reshape(mask_shape),
            head_part,
            jnp.where(last_rows.reshape(mask_shape), tail_part, 0.0),
        )

    hidden0 = layer_input.astype(jnp.float32)
    normed1_out, normed1, inverse1 = layer_norm(hidden0, norm1_gain, norm1_shift)
    first_act = normed1_out.astype(jnp.bfloat16)
    proj_qkv = jnp.einsum(
        "mtd,dcf->mtcf", first_act, w_qkv, preferred_element_type=jnp.float32
    ).astype(jnp.bfloat16)
    keys_vals = proj_qkv[:, :, 1:]
    keep_all = key_keep.astype(jnp.float32).reshape(batches, blocks_all, BLOCK)
    keep_padded = jnp.pad(keep_all, ((0, 0), (1, 1), (0, 0)))
    keep_window = lax.dynamic_slice_in_dim(keep_padded, myself * blocks_dev, blocks_dev + 2, 1)
    keep_here = keep_window[:, 1 : blocks_dev + 1].reshape(batches, tokens_dev)
    sliding_keep = jnp.concatenate(
        [
            keep_window[:, 0:blocks_dev],
            keep_window[:, 1 : blocks_dev + 1],
            keep_window[:, 2 : blocks_dev + 2],
        ],
        axis=2,
    )
    lead_pair = jnp.concatenate([keep_all[:, 0], keep_all[:, blocks_all - 1]], axis=1)
    lead_keep = jnp.broadcast_to(
        lead_pair.reshape(batches, 1, lead_len), (batches, blocks_dev, lead_len)
    )
    extended = with_halo(keys_vals, (("seq", 1),), BLOCK)
    ext_blocks = extended.reshape(batches, blocks_dev + 2, BLOCK, 2, local_width)
    sliding = jnp.concatenate(
        [
            ext_blocks[:, 0:blocks_dev],
            ext_blocks[:, 1 : blocks_dev + 1],
            ext_blocks[:, 2 : blocks_dev + 2],
        ],
        axis=2,
    )
    ends = []
    for root in (0, devices - 1):
        piece = proj_qkv[:, :BLOCK] if root == 0 else proj_qkv[:, pad_rows:]
        ends.append(spread(piece, "seq", root))
    leading = jnp.concatenate(ends, axis=1)
    lead_kv = jnp.broadcast_to(
        leading[:, None, :, 1:], (batches, blocks_dev, lead_len, 2, local_width)
    )
    ref_table = (
        rand_blocks.reshape(batches, devices, blocks_dev, RANDS)
        .transpose(1, 0, 2, 3)
        .reshape(devices, ref_count)
    )
    owners = ref_table // blocks_dev
    within = ref_table - owners * blocks_dev
    batch_of = jnp.arange(ref_count, dtype=jnp.int32) // (blocks_dev * RANDS)
    source_row = batch_of[None, :] * blocks_dev + within
    positions = jnp.arange(ref_count, dtype=jnp.int32)
    before = positions[None, :] < positions[:, None]
    slot_rank = jnp.sum(
        ((owners[:, :, None] == owners[:, None, :]) & before[None]).astype(jnp.int32), -1
    )
    chosen = (owners == myself)[:, :, None] & (
        slot_rank[:, :, None] == jnp.arange(slots_per, dtype=jnp.int32)[None, None, :]
    )
    row_onehot = (
        source_row[:, :, None] == jnp.arange(batches * blocks_dev, dtype=jnp.int32)[None, None, :]
    )
    selector = jnp.einsum(
        "sic,sik->sck", chosen.astype(jnp.float32), row_onehot.astype(jnp.float32), precision=HIGH
    ).reshape(devices * slots_per, batches * blocks_dev)
    own_blocks = keys_vals.reshape(batches * blocks_dev, BLOCK * 2 * local_width)
    outgoing = jnp.dot(
        selector.astype(jnp.bfloat16), own_blocks, preferred_element_type=jnp.float32
    ).astype(jnp.bfloat16)
    mine_owner = lax.dynamic_index_in_dim(owners, myself, 0, keepdims=False)
    mine_rank = lax.dynamic_index_in_dim(slot_rank, myself, 0, keepdims=False)
    picker = (
        (mine_owner * slots_per + mine_rank)[:, None]
        == jnp.arange(devices * slots_per, dtype=jnp.int32)[None, :]
    ).astype(jnp.float32)
    mine_ids = lax.dynamic_index_in_dim(ref_table, myself, 0, keepdims=False)
    id_onehot = (
        mine_ids.reshape(batches, blocks_dev * RANDS)[:, :, None]
        == jnp.arange(blocks_all, dtype=jnp.int32)[None, None, :]
    ).astype(jnp.float32)
    random_keep = jnp.einsum("mjn,mnb->mjb", id_onehot, keep_all, precision=HIGH).reshape(
        batches, blocks_dev, RANDS * BLOCK
    )
    weight_rows = jnp.concatenate([sliding_keep, lead_keep, random_keep], axis=2)

    def fetch(arrived):
        picked = jnp.dot(
            picker.astype(jnp.bfloat16), arrived, preferred_element_type=jnp.float32
        ).astype(jnp.bfloat16)
        return picked.reshape(batches, blocks_dev, RANDS * BLOCK, 2, local_width)

    def assemble(random_part):
        listed = jnp.concatenate([sliding, lead_kv, random_part], axis=2)
        shape = (batches, blocks_dev, listed.shape[2], heads_here, HEAD_DIM)
        return (listed[:, :, :, 0].reshape(shape), listed[:, :, :, 1].reshape(shape))

    incoming = lax.all_to_all(outgoing, "seq", split_axis=0, concat_axis=0, tiled=True)
    key_rows, value_rows = assemble(fetch(incoming))
    queries = proj_qkv[:, :, 0].reshape(batches, blocks_dev, BLOCK, heads_here, HEAD_DIM)
    scores = (
        jnp.einsum("mbqhd,mbkhd->mbhqk", queries, key_rows, preferred_element_type=jnp.float32)
        * inv_root
    )
    row_top = jnp.max(scores, -1, keepdims=True)
    expo_rows = jnp.exp(scores - row_top) * weight_rows[:, :, None, None, :]
    denom_sum = jnp.sum(expo_rows, -1, keepdims=True)
    prob_low = (expo_rows / denom_sum).astype(jnp.bfloat16)
    log_total = row_top + jnp.log(denom_sum)
    sparse = jnp.einsum(
        "mbhqk,mbkhd->mbqhd", prob_low, value_rows, preferred_element_type=jnp.float32
    ).reshape(batches, tokens_dev, local_width)
    lead_q = leading[:, :, 0].reshape(lead_shape)
    local_keys = proj_qkv[:, :, 1].reshape(head_shape)
    local_values = proj_qkv[:, :, 2].reshape(head_shape)
    lead_scores = (
        jnp.einsum("mqhd,mkhd->mhqk", lead_q, local_keys, preferred_element_type=jnp.float32)
        * inv_root
    )
    lead_top = jnp.max(lead_scores, -1)
    lead_expo = jnp.exp(lead_scores - lead_top[..., None]) * keep_here[:, None, None, :]
    lead_sum = jnp.sum(lead_expo, -1)
    lead_acc = jnp.einsum(
        "mhqk,mkhd->mhqd", lead_expo, local_values.astype(jnp.float32), precision=HIGH
    )
    glob_top, glob_sum, glob_acc = combined_all((lead_top, lead_sum, lead_acc), "seq", join_rows)
    glob_heads = glob_acc / glob_sum[..., None]
    glob_lse = glob_top + jnp.log(glob_sum)
    glob_out = glob_heads.transpose(0, 2, 1, 3).reshape(batches, lead_len, local_width)
    attn_mixed = jnp.where(is_lead[None, :, None], place(glob_out), sparse).astype(jnp.bfloat16)
    attn_part = jnp.einsum("mtf,df->mtd", attn_mixed, w_out, preferred_element_type=jnp.float32)
    hidden1 = hidden0 + head_total(attn_part)
    normed2_out, normed2, inverse2 = layer_norm(hidden1, norm2_gain, norm2_shift)
    second_act = normed2_out.astype(jnp.bfloat16)
    hidden1_share = own_share(hidden1)
    pre_act = jnp.einsum("mtd,df->mtf", second_act, w_up, preferred_element_type=jnp.float32)
    up_full, gelu_pull = jax.vjp(partial(jax.nn.gelu, approximate=False), pre_act)
    up_act = up_full.astype(jnp.bfloat16)
    ffn_part = jnp.einsum("mtf,df->mtd", up_act, w_down, preferred_element_type=jnp.float32)
    layer_output = hidden1_share + own_share(head_total(ffn_part))
    grad_output = out_grad.astype(jnp.float32)
    grad_w_down = jnp.einsum("mtd,mtf->df", out_grad, up_act, preferred_element_type=jnp.float32)
    grad_up = jnp.einsum("mtd,df->mtf", out_grad, w_down, preferred_element_type=jnp.float32)
    grad_pre = gelu_pull(grad_up)[0].astype(jnp.bfloat16)
    grad_w_up = jnp.einsum("mtd,mtf->df", second_act, grad_pre, preferred_element_type=jnp.float32)
    second_back = jnp.einsum("mtf,df->mtd", grad_pre, w_up, preferred_element_type=jnp.float32)
    back_second, grad_gain2, grad_shift2 = norm_back(
        head_total(second_back), normed2, inverse2, norm2_gain
    )
    grad_hidden1 = grad_output + back_second
    grad_attn = grad_hidden1.astype(jnp.bfloat16)
    grad_hidden1_share = own_share(grad_hidden1)
    grad_w_out = jnp.einsum(
        "mtd,mtf->df", grad_attn, attn_mixed, preferred_element_type=jnp.float32
    )
    grad_mixed = jnp.einsum(
        "mtd,df->mtf", grad_attn, w_out, preferred_element_type=jnp.float32
    ).astype(jnp.bfloat16)
    resent = lax.all_to_all(outgoing, "seq", split_axis=0, concat_axis=0, tiled=True)
    key_back, value_back = assemble(fetch(resent))
    grad_heads = jnp.where(is_lead[None, :, None], jnp.zeros_like(grad_mixed), grad_mixed).reshape(
        batches, blocks_dev, BLOCK, heads_here, HEAD_DIM
    )
    scores_back = (
        jnp.einsum("mbqhd,mbkhd->mbhqk", queries, key_back, preferred_element_type=jnp.float32)
        * inv_root
    )
    prob_back = jnp.exp(scores_back - log_total) * weight_rows[:, :, None, None, :]
    grad_probs = jnp.einsum(
        "mbqhd,mbkhd->mbhqk", grad_heads, value_back, preferred_element_type=jnp.float32
    )
    row_delta = jnp.sum(prob_back * grad_probs, -1, keepdims=True)
    grad_scores = (prob_back * (grad_probs - row_delta)).astype(jnp.bfloat16)
    grad_query = (
        jnp.einsum("mbhqk,mbkhd->mbqhd", grad_scores, key_back, preferred_element_type=jnp.float32)
        * inv_root
    )
    grad_key = (
        jnp.einsum("mbhqk,mbqhd->mbkhd", grad_scores, queries, preferred_element_type=jnp.float32)
        * inv_root
    )
    grad_value = jnp.einsum(
        "mbhqk,mbqhd->mbkhd",
        prob_back.astype(jnp.bfloat16),
        grad_heads,
        preferred_element_type=jnp.float32,
    )
    listed_len = grad_key.shape[2]
    grad_kv = jnp.stack(
        [
            grad_key.reshape(batches, blocks_dev, listed_len, local_width),
            grad_value.reshape(batches, blocks_dev, listed_len, local_width),
        ],
        axis=3,
    )
    slide_grad = grad_kv[:, :, : 3 * BLOCK].reshape(batches, blocks_dev, 3, BLOCK, 2, local_width)
    ext_grad = sum(
        (
            jnp.pad(
                slide_grad[:, :, offset], ((0, 0), (offset, 2 - offset), (0, 0), (0, 0), (0, 0))
            )
            for offset in range(3)
        )
    )
    rim_grads = jnp.concatenate([ext_grad[:, 0], ext_grad[:, blocks_dev + 1]], axis=1)
    returned = with_halo(rim_grads.astype(jnp.bfloat16), (("seq", 1),), BLOCK).astype(
        rim_grads.dtype
    )
    own_grad = ext_grad[:, 1 : blocks_dev + 1]
    own_grad = own_grad.at[:, 0].add(returned[:, :BLOCK])
    own_grad = own_grad.at[:, blocks_dev - 1].add(returned[:, 3 * BLOCK :])
    lead_part = jnp.sum(grad_kv[:, :, 3 * BLOCK : 5 * BLOCK], axis=1)
    random_grad = grad_kv[:, :, 5 * BLOCK :].reshape(ref_count, BLOCK * 2 * local_width)
    slot_grads = jnp.dot(picker.T, random_grad, precision=HIGH)
    arrived_grads = lax.all_to_all(
        slot_grads.astype(jnp.bfloat16), "seq", split_axis=0, concat_axis=0, tiled=True
    ).astype(slot_grads.dtype)
    own_random = jnp.dot(selector.T, arrived_grads, precision=HIGH).reshape(
        batches, blocks_dev, BLOCK, 2, local_width
    )
    own_grad = own_grad + own_random
    lead_rows = []
    for root in (0, devices - 1):
        piece = grad_mixed[:, :BLOCK] if root == 0 else grad_mixed[:, pad_rows:]
        lead_rows.append(spread(piece, "seq", root))
    sent_heads = jnp.concatenate(lead_rows, axis=1).reshape(lead_shape)
    lead_delta = jnp.einsum(
        "mqhd,mhqd->mhq", sent_heads.astype(jnp.float32), glob_heads, precision=HIGH
    )
    lead_probs = jnp.exp(lead_scores - glob_lse[..., None]) * keep_here[:, None, None, :]
    lead_dp = jnp.einsum(
        "mqhd,mkhd->mhqk", sent_heads, local_values, preferred_element_type=jnp.float32
    )
    lead_ds = (lead_probs * (lead_dp - lead_delta[..., None])).astype(jnp.bfloat16)
    part_query = (
        jnp.einsum("mhqk,mkhd->mqhd", lead_ds, local_keys, preferred_element_type=jnp.float32)
        * inv_root
    )
    lead_dk = (
        jnp.einsum("mhqk,mqhd->mkhd", lead_ds, lead_q, preferred_element_type=jnp.float32)
        * inv_root
    )
    lead_dv = jnp.einsum(
        "mhqk,mqhd->mkhd", lead_probs, sent_heads.astype(jnp.float32), precision=HIGH
    )
    sum_query, sum_kv = lax.psum(
        (part_query.reshape(batches, lead_len, local_width), lead_part), "seq"
    )
    query_total = grad_query.reshape(batches, tokens_dev, local_width) + place(sum_query)
    kv_total = own_grad.reshape(batches, tokens_dev, 2, local_width)
    kv_total = kv_total + jnp.stack(
        [
            lead_dk.reshape(batches, tokens_dev, local_width),
            lead_dv.reshape(batches, tokens_dev, local_width),
        ],
        axis=2,
    )
    kv_total = kv_total + place(sum_kv)
    grad_qkv = jnp.concatenate([query_total[:, :, None], kv_total], axis=2).astype(jnp.bfloat16)
    grad_w_qkv = jnp.einsum(
        "mtd,mtcf->dcf", first_act, grad_qkv, preferred_element_type=jnp.float32
    )
    first_back = jnp.einsum("mtcf,dcf->mtd", grad_qkv, w_qkv, preferred_element_type=jnp.float32)
    back_first, grad_gain1, grad_shift1 = norm_back(
        head_total(first_back), normed1, inverse1, norm1_gain
    )
    input_grad = grad_hidden1_share + own_share(back_first)
    summed = (
        lax.psum_scatter(grad_w_qkv, "seq", scatter_dimension=0, tiled=True),
        lax.psum_scatter(grad_w_out, "seq", scatter_dimension=0, tiled=True),
        lax.psum_scatter(grad_w_up, "seq", scatter_dimension=0, tiled=True),
        lax.psum_scatter(grad_w_down, "seq", scatter_dimension=0, tiled=True),
        lax.psum_scatter(grad_gain1, "seq", scatter_dimension=0, tiled=True),
        lax.psum_scatter(grad_shift1, "seq", scatter_dimension=0, tiled=True),
        lax.psum_scatter(grad_gain2, "seq", scatter_dimension=0, tiled=True),
        lax.psum_scatter(grad_shift2, "seq", scatter_dimension=0, tiled=True),
    )
    return (
        layer_output,
        input_grad,
        summed[0],
        summed[1],
        summed[2],
        summed[3],
        summed[4],
        summed[5],
        summed[6],
        summed[7],
    )


def solution(mesh):
    return jax.shard_map(
        per_device,
        mesh=mesh,
        in_specs=(
            P(None, "seq", None),
            P(None, "seq", None),
            P(),
            P(),
            P(None, None, "tp"),
            P(None, "tp"),
            P(),
            P(),
            P(None, "tp"),
            P(None, "tp"),
            P(),
            P(),
        ),
        out_specs=(
            P(None, ("seq", "tp"), None),
            P(None, ("seq", "tp"), None),
            P("seq", None, "tp"),
            P("seq", "tp"),
            P("seq", "tp"),
            P("seq", "tp"),
            P("seq"),
            P("seq"),
            P("seq"),
            P("seq"),
        ),
        check_vma=False,
    )
```

profile of v0, /device:TPU:0, one launch (start us, length us, event | category | flops | bytes accessed | tf_op | source)
XLA Modules:
  0.0 1227.9 jit_solution(12847360623724683897)
XLA Ops:
  83.4 79.6 %all-reduce.36.cloned.1.call-done = (bf16[2,64,3,192]{1,3,2,0:T(8,128)(2,1)}, bf16[2,64,3,192]{1,3,2,0:T(8,128)(2,1)}) async-done(((bf16[2,64,3,192]{1,3,2,0:T(8,128)(2,1)}, bf16[2,64,3,192]{1,3,2,0:T(8,128)(2,1)}), (bf16[2,64,3,192]{1,3,2,0:T(8,128)(2,1)}, bf16[2,64,3,192]{1,3,2,0:T(8,128)(2,1)})) %all-reduce.36.cloned.1.call-update) | async-done | bytes 294928 | tf_op jit(solution)/shard_map/psum | solution.py:33
  167.1 32.2 %all-gather.2 = bf16[16,3,128,64]{2,3,1,0:T(8,128)(2,1)S(1)} all-gather(bf16[2,3,128,64]{2,3,1,0:T(8,128)(2,1)S(1)} %fusion.43), channel_id=4, replica_groups=mesh['seq'=8,'tp'=4] {'seq'}, dimensions={0}, use_global_device_ids=true | all-gather | bytes 884736 | tf_op jit(solution)/shard_map/all_gather | solution.py:38
  200.4 26.0 %all-gather.1 = bf16[16,3,128]{2,1,0:T(4,128)(2,1)S(1)} all-gather(bf16[2,3,128]{2,1,0:T(4,128)(2,1)S(1)} %fusion.34), channel_id=3, replica_groups=mesh['seq'=8,'tp'=4] {'seq'}, dimensions={0}, use_global_device_ids=true | all-gather | bytes 13824 | tf_op jit(solution)/shard_map/all_gather | solution.py:38
  226.4 26.3 %all-gather = bf16[16,3,128]{2,1,0:T(4,128)(2,1)S(1)} all-gather(bf16[2,3,128]{2,1,0:T(4,128)(2,1)} %convert_element_type.190), channel_id=2, replica_groups=mesh['seq'=8,'tp'=4] {'seq'}, dimensions={0}, use_global_device_ids=true | all-gather | bytes 13824 | tf_op jit(solution)/shard_map/all_gather | solution.py:38
  252.7 10.6 while.21
  289.5 17.7 %fusion.103 = (bf16[2,8,512,1,192]{4,3,2,1,0:T(2,128)(2,1)}, bf16[2,8,512,1,192]{4,3,2,1,0:T(2,128)(2,1)}) fusion(bf16[2,8,512,2,192]{4,3,2,1,0:T(2,128)(2,1)} %constant_dynamic-update-slice_fusion), kind=kLoop, calls=%fused_computation.236 | loop fusion | bytes 12582912 | tf_op jit(solution)/shard_map/slice | solution.py:233
  307.2 19.7 %copy.206 = bf16[2,8,512,1,192]{2,4,1,0,3:T(8,128)(2,1)} copy(bf16[2,8,512,1,192]{4,3,2,1,0:T(2,128)(2,1)} %get-tuple-element.349) | data formatting | bytes 6291456 | tf_op jit(solution)/shard_map/slice | solution.py:233
  326.9 19.8 %copy.205 = bf16[2,8,512,1,192]{2,4,1,0,3:T(8,128)(2,1)} copy(bf16[2,8,512,1,192]{4,3,2,1,0:T(2,128)(2,1)} %get-tuple-element.350) | data formatting | bytes 6291456 | tf_op jit(solution)/shard_map/slice | solution.py:233
  363.7 65.9 %all-reduce.26.cloned.1.call-done = f32[2,512,768]{2,1,0:T(8,128)} async-done(((f32[2,512,768]{2,1,0:T(8,128)}), f32[2,512,768]{2,1,0:T(8,128)}) %all-reduce.26.cloned.1.call-update) | async-done | bytes 3145744 | tf_op jit(solution)/shard_map/psum | solution.py:127
  434.9 8.3 multiply_convert_fusion.1
  456.1 62.2 %all-reduce.28.cloned.1.call-done = f32[2,512,768]{2,1,0:T(8,128)} async-done(((f32[2,512,768]{2,1,0:T(8,128)}), f32[2,512,768]{2,1,0:T(8,128)}) %all-reduce.28.cloned.1.call-update) | async-done | bytes 3145744 | tf_op jit(solution)/shard_map/psum | solution.py:127
  537.6 8.3 copy.216
  556.7 8.2 copy.215
  564.9 8.2 fusion.3
  573.1 10.3 copy.223
  583.4 9.5 reshape.438
  643.2 71.6 %all-reduce.34.cloned.1.call-done = (bf16[2,64,192]{1,2,0:T(8,128)(2,1)}, bf16[2,64,192]{1,2,0:T(8,128)(2,1)}) async-done(((bf16[2,64,192]{1,2,0:T(8,128)(2,1)}, bf16[2,64,192]{1,2,0:T(8,128)(2,1)}), (bf16[2,64,192]{1,2,0:T(8,128)(2,1)}, bf16[2,64,192]{1,2,0:T(8,128)(2,1)})) %all-reduce.34.cloned.1.call-update) | async-done | bytes 98320 | tf_op jit(solution)/shard_map/psum | solution.py:33
  738.2 55.7 %all-reduce.30.cloned.1.call-done = (f32[2,128,2,192]{1,3,2,0:T(8,128)}, f32[2,128,192]{1,2,0:T(8,128)}) async-done(((f32[2,128,2,192]{1,3,2,0:T(8,128)}, f32[2,128,192]{1,2,0:T(8,128)}), (f32[2,128,2,192]{1,3,2,0:T(8,128)}, f32[2,128,192]{1,2,0:T(8,128)})) %all-reduce.30.cloned.1.call-update) | async-done | bytes 589840 | tf_op jit(solution)/shard_map/psum | solution.py:383
  841.9 95.7 %all-reduce.32.cloned.1.call-done = (f32[2,512,768]{2,1,0:T(8,128)}, f32[2,512,768]{2,1,0:T(8,128)}) async-done(((f32[2,512,768]{2,1,0:T(8,128)}, f32[2,512,768]{2,1,0:T(8,128)}), (f32[2,512,768]{2,1,0:T(8,128)}, f32[2,512,768]{2,1,0:T(8,128)})) %all-reduce.32.cloned.1.call-update) | async-done | bytes 6291472 | tf_op jit(solution)/shard_map/psum | solution.py:127
  942.6 37.3 %all-reduce.14 = (f32[768]{0:T(1024)S(1)}, f32[768]{0:T(1024)S(1)}, f32[768]{0:T(1024)S(1)}, f32[768]{0:T(1024)S(1)}) all-reduce(f32[768]{0:T(1024)S(1)} %get-tuple-element.305, f32[768]{0:T(1024)S(1)} %get-tuple-element.304, f32[768]{0:T(1024)S(1)} %copy-done.60, f32[768]{0:T(1024)S(1)} %copy-done.61), channel_id=9, replica_groups=mesh['seq'=8,'tp'=4] {'seq'}, use_global_device_ids=true, to_apply=%region_32.33.clone | all-reduce | flops 3072 | bytes 24576
  987.3 17.3 %reduce-scatter.9.cloned.1.call-done = f32[96,192]{1,0:T(8,128)} async-done(((f32[768,192]{1,0:T(8,128)}), f32[96,192]{1,0:T(8,128)}) %reduce-scatter.9.cloned.1.call-update) | async-done | bytes 73744 | tf_op jit(solution)/shard_map/reduce_scatter | solution.py:407
  1004.6 72.1 %reduce-scatter.11.cloned.1.call-done = f32[96,768]{1,0:T(8,128)} async-done(((f32[768,768]{1,0:T(8,128)}), f32[96,768]{1,0:T(8,128)}) %reduce-scatter.11.cloned.1.call-update) | async-done | bytes 294928 | tf_op jit(solution)/shard_map/reduce_scatter | solution.py:408
  1076.7 72.2 %reduce-scatter.13.cloned.1.call-done = f32[96,768]{1,0:T(8,128)} async-done(((f32[768,768]{1,0:T(8,128)}), f32[96,768]{1,0:T(8,128)}) %reduce-scatter.13.cloned.1.call-update) | async-done | bytes 294928
  1148.9 71.9 %reduce-scatter.7.cloned.1.call-done = f32[96,3,192]{2,0,1:T(8,128)} async-done(((f32[768,3,192]{2,0,1:T(8,128)}), f32[96,3,192]{2,0,1:T(8,128)}) %reduce-scatter.7.cloned.1.call-update) | async-done | bytes 221200 | tf_op jit(solution)/shard_map/reduce_scatter | solution.py:406
  (381 shorter events, 315.6 us)
Async XLA Ops:
  7.2 425.3 %copy-start = (bf16[768,768]{1,0:T(8,128)(2,1)S(1)}, bf16[768,768]{1,0:T(8,128)(2,1)}, u32[]{:S(2)}) copy-start(bf16[768,768]{1,0:T(8,128)(2,1)} %param.26) | copy-start | bytes 3538948
  13.5 56.4 %collective-permute-start = (bf16[2,64,2,192]{1,3,2,0:T(8,128)(2,1)}, bf16[2,64,2,192]{1,3,2,0:T(8,128)(2,1)}, u32[]{:S(2)}, u32[]{:S(2)}) collective-permute-start(bf16[2,64,2,192]{1,3,2,0:T(8,128)(2,1)} %get-tuple-element.368), channel_id=1, source_target_pairs={{0,4},{4,8},{8,12},{12,16},{16,20},{20,24},{24,28},{1,5},{5,9},{9,... | collective-permute-start | bytes 294920 | tf_op jit(solution)/shard_map/ppermute | solution.py:23
  19.0 50.8 %collective-permute-start.1 = (bf16[2,64,2,192]{1,3,2,0:T(8,128)(2,1)}, bf16[2,64,2,192]{1,3,2,0:T(8,128)(2,1)}, u32[]{:S(2)}, u32[]{:S(2)}) collective-permute-start(bf16[2,64,2,192]{1,3,2,0:T(8,128)(2,1)} %get-tuple-element.369), channel_id=1, source_target_pairs={{4,0},{8,4},{12,8},{16,12},{20,16},{24,20},{28,24},{5,1},{9,5},{13... | collective-permute-start | bytes 294920 | tf_op jit(solution)/shard_map/ppermute | solution.py:26
  39.1 231.2 %all-to-all-start = ((bf16[8,6,24576]{2,1,0:T(8,128)(2,1)}), bf16[8,6,24576]{2,1,0:T(8,128)(2,1)}, u32[]{:S(2)}, u32[]{:S(2)}) async-start(bf16[8,6,24576]{2,1,0:T(8,128)(2,1)} %all_to_all.17), calls=%async_computation | async-start | bytes 6291456 | tf_op jit(solution)/shard_map/all_to_all | solution.py:235
  46.1 116.9 %all-reduce.36.cloned.1.call-start = ((), (), s32[]{:S(2)}) async-start(), calls=%async_computation.15 | async-start | bytes 1179648 | tf_op jit(solution)/shard_map/psum | solution.py:33
  48.1 381.5 %all-reduce.26.cloned.1.call-start = ((), (), s32[]{:S(2)}) async-start(), calls=%async_computation.6 | async-start | bytes 6291456 | tf_op jit(solution)/shard_map/psum | solution.py:127
  54.1 304.3 %copy-start.62 = (pred[512]{0:T(512)(128)(4,1)}, pred[512]{0:T(512)(128)(4,1)S(1)}, u32[]{:S(2)}) copy-start(pred[512]{0:T(512)(128)(4,1)S(1)} %get-tuple-element.396) | copy-start | bytes 1540
  77.3 86.8 %copy-start.23 = (bf16[2,512,1,192]{1,3,2,0:T(8,128)(2,1)S(1)}, bf16[2,512,1,192]{1,3,2,0:T(8,128)(2,1)}, u32[]{:S(2)}) copy-start(bf16[2,512,1,192]{1,3,2,0:T(8,128)(2,1)} %get-tuple-element.365) | copy-start | bytes 1179652
  81.4 84.5 %copy-start.25 = (bf16[2,512,1,192]{1,3,2,0:T(8,128)(2,1)S(1)}, bf16[2,512,1,192]{1,3,2,0:T(8,128)(2,1)}, u32[]{:S(2)}) copy-start(bf16[2,512,1,192]{1,3,2,0:T(8,128)(2,1)} %get-tuple-element.363) | copy-start | bytes 1179652
  363.7 154.6 %all-reduce.28.cloned.1.call-start = ((), (), s32[]{:S(2)}) async-start(), calls=%async_computation.7 | async-start | bytes 6291456 | tf_op jit(solution)/shard_map/psum | solution.py:127
  432.7 89.9 %copy-start.49 = (f32[2,512]{1,0:T(2,128)}, f32[2,512]{1,0:T(2,128)S(1)}, u32[]{:S(2)}) copy-start(f32[2,512]{1,0:T(2,128)S(1)} %add_rsqrt_fusion) | copy-start | bytes 12292
  600.0 198.0 %all-to-all-start.1 = ((bf16[8,6,24576]{2,1,0:T(8,128)(2,1)}), bf16[8,6,24576]{2,1,0:T(8,128)(2,1)}, u32[]{:S(2)}, u32[]{:S(2)}) async-start(bf16[8,6,24576]{2,1,0:T(8,128)(2,1)} %all_to_all.20), calls=%async_computation.1 | async-start | bytes 6291456 | tf_op jit(solution)/shard_map/all_to_all | solution.py:352
  605.5 109.3 %all-reduce.34.cloned.1.call-start = ((), (), s32[]{:S(2)}) async-start(), calls=%async_computation.14 | async-start | bytes 393216 | tf_op jit(solution)/shard_map/psum | solution.py:33
  617.5 176.3 %all-reduce.30.cloned.1.call-start = ((), (), s32[]{:S(2)}) async-start(), calls=%async_computation.12 | async-start | bytes 1179648 | tf_op jit(solution)/shard_map/psum | solution.py:383
  633.4 82.6 %collective-permute-start.2 = (bf16[2,64,2,192]{3,2,1,0:T(2,128)(2,1)S(1)}, bf16[2,64,2,192]{3,2,1,0:T(2,128)(2,1)}, u32[]{:S(2)}, u32[]{:S(2)}) collective-permute-start(bf16[2,64,2,192]{3,2,1,0:T(2,128)(2,1)S(1)} %get-tuple-element.358), channel_id=1, source_target_pairs={{0,4},{4,8},{8,12},{12,16},{16,20},{20,24},{24,28},{1,5},{5,9},{9,... | collective-permute-start | bytes 294920 | tf_op jit(solution)/shard_map/ppermute | solution.py:23
  637.9 78.1 %collective-permute-start.3 = (bf16[2,64,2,192]{3,2,1,0:T(2,128)(2,1)S(1)}, bf16[2,64,2,192]{3,2,1,0:T(2,128)(2,1)}, u32[]{:S(2)}, u32[]{:S(2)}) collective-permute-start(bf16[2,64,2,192]{3,2,1,0:T(2,128)(2,1)S(1)} %get-tuple-element.359), channel_id=1, source_target_pairs={{4,0},{8,4},{12,8},{16,12},{20,16},{24,20},{28,24},{5,1},{9,5},{13... | collective-permute-start | bytes 294920 | tf_op jit(solution)/shard_map/ppermute | solution.py:26
  639.2 80.7 %copy-start.6 = (f32[2,3,128,512]{3,2,1,0:T(8,128)S(1)}, f32[2,3,128,512]{3,2,1,0:T(8,128)}, u32[]{:S(2)}) copy-start(f32[2,3,128,512]{3,2,1,0:T(8,128)} %copy-done.5) | copy-start | bytes 4718596
  639.2 80.7 %copy-start.26 = (bf16[2,512,1,192]{1,3,2,0:T(8,128)(2,1)S(1)}, bf16[2,512,1,192]{1,3,2,0:T(8,128)(2,1)}, u32[]{:S(2)}) copy-start(bf16[2,512,1,192]{1,3,2,0:T(8,128)(2,1)} %get-tuple-element.363) | copy-start | bytes 1179652
  721.6 216.0 %all-reduce.32.cloned.1.call-start = ((), (), s32[]{:S(2)}) async-start(), calls=%async_computation.13 | async-start | bytes 12582912 | tf_op jit(solution)/shard_map/psum | solution.py:127
  818.8 185.8 %reduce-scatter.9.cloned.1.call-start = ((), (), s32[]{:S(2)}) async-start(), calls=%async_computation.9 | async-start | bytes 884736 | tf_op jit(solution)/shard_map/reduce_scatter | solution.py:407
  823.1 253.5 %reduce-scatter.11.cloned.1.call-start = ((), (), s32[]{:S(2)}) async-start(), calls=%async_computation.10 | async-start | bytes 2654208 | tf_op jit(solution)/shard_map/reduce_scatter | solution.py:408
  829.6 319.2 %reduce-scatter.13.cloned.1.call-start = ((), (), s32[]{:S(2)}) async-start(), calls=%async_computation.11 | async-start | bytes 2654208
  837.3 383.5 %reduce-scatter.7.cloned.1.call-start = ((), (), s32[]{:S(2)}) async-start(), calls=%async_computation.8 | async-start | bytes 2654208 | tf_op jit(solution)/shard_map/reduce_scatter | solution.py:406
  937.6 283.2 %copy-start.1 = (bf16[768,768]{1,0:T(8,128)(2,1)S(1)}, bf16[768,768]{1,0:T(8,128)(2,1)}, u32[]{:S(2)}) copy-start(bf16[768,768]{1,0:T(8,128)(2,1)} %param.26) | copy-start | bytes 3538948
  (77 other events, 726.5 us)
Sparse Core Ops, SparseCore 0:
  50.9 112.0 all-reduce.35
  363.8 65.7 all-reduce.25
  449.8 68.5 all-reduce.27
  617.6 97.1 all-reduce.33
  721.7 72.0 all-reduce.29
  818.9 118.7 all-reduce.31
  941.8 62.7 reduce-scatter.8
  1008.7 67.9 reduce-scatter.10
  1080.8 68.0 reduce-scatter.12
  1152.8 67.9 reduce-scatter.6
where the time goes:
time: 1240 us; the launch traced here: 1230 us
  waiting for transfers between devices  664 us (54%)
  local copies, waits for them, and re-layouts  228 us (18%)
  blocking collectives  122 us (10%)
  matrix products  87.1 us (7%)
  other arithmetic  84.1 us (7%)
  starting transfers between devices  26.2 us (2%)
  between operations  16.2 us (1%)
    psum x3, waiting for transfers between devices, head_total(): return lax.psum(value, 'tp')  224 us
    psum x2, waiting for transfers between devices, spread(): return lax.psum(block, axis)  151 us
    all_gather x3, blocking collectives, combined_all(): lax.all_gather(a.astype(kind), axis)  84.5 us
    unnamed x11, waiting for transfers between devices  72.3 us
    reduce_scatter x1, waiting for transfers between devices, per_device(): lax.psum_scatter(grad_w_up, 'seq', scatter_dimension=0, tiled=True)  72.1 us
    reduce_scatter x1, waiting for transfers between devices, per_device(): lax.psum_scatter(grad_w_qkv, 'seq', scatter_dimension=0, tiled=True)  71.9 us
    psum x1, waiting for transfers between devices, per_device(): lax.psum((part_query.reshape(batches, lead_len, local_width), lead_part),...  55.7 us
    slice x2, local copies, waits for them, and re-layouts, assemble(): listed[:, :, :, 0].reshape(shape)  37.4 us
  transfers between devices with their start and end apart: 16, of which 10 were waited for; matrix products, arithmetic and copies ran while one was open for 14% of the time, Pallas kernels for 0%

commit v1 on v0

v1 whole, which is shorter than its diff:
```python
from functools import partial
import math

import jax
import jax.numpy as jnp
from jax import lax
from jax.experimental import pallas as pl
from jax.experimental.pallas import tpu as pltpu
from jax.sharding import PartitionSpec as P

HD = 64
BLOCK = 64
RANDS = 3
EPS = 1e-06
SWAP = (0, 2, 1, 3)
NEG = -1e30
F32 = jnp.float32
BF16 = jnp.bfloat16
VMEM = pl.BlockSpec(memory_space=pltpu.VMEM)
SMEM = pl.BlockSpec(memory_space=pltpu.SMEM)
PARAMS = pltpu.CompilerParams(vmem_limit_bytes=56 * 1024 * 1024)


def sds(shape, kind):
    return jax.ShapeDtypeStruct(shape, kind)


def call(body, outs, scratch=(), name=None):
    def run(*args, smem=()):
        specs = [SMEM] * len(smem) + [VMEM] * len(args)
        return pl.pallas_call(
            body,
            out_shape=outs,
            in_specs=specs,
            out_specs=jax.tree.map(lambda _: VMEM, outs),
            scratch_shapes=list(scratch),
            compiler_params=PARAMS,
            name=name,
        )(*smem, *args)

    return run


def dot_nt(a, b):
    return lax.dot_general(a, b, (((1,), (1,)), ((), ())), preferred_element_type=F32)


def dot_tn(a, b):
    return lax.dot_general(a, b, (((0,), (0,)), ((), ())), preferred_element_type=F32)


def dot_nn(a, b):
    return lax.dot_general(a, b, (((1,), (0,)), ((), ())), preferred_element_type=F32)


def two_heads(tile):
    lane = lax.broadcasted_iota(jnp.int32, tile.shape, 1)
    zero = jnp.zeros_like(tile)
    return jnp.concatenate([jnp.where(lane < HD, tile, zero), jnp.where(lane >= HD, tile, zero)], 0)


def pick_heads(pair, rows):
    lane = lax.broadcasted_iota(jnp.int32, (rows, 2 * HD), 1)
    return jnp.where(lane < HD, pair[:rows], pair[rows:])


def half(tile, upper):
    lane = lax.broadcasted_iota(jnp.int32, tile.shape, 1)
    return jnp.where((lane >= HD) if upper else (lane < HD), tile, jnp.zeros_like(tile))


def lanes_of(columns, rows):
    lane = lax.broadcasted_iota(jnp.int32, (rows, 2 * HD), 1)
    out = jnp.zeros((rows, 2 * HD), F32)
    for at, column in enumerate(columns):
        out = jnp.where(lane == at, column, out)
    return out


def hi_lo(value):
    hi = value.astype(BF16).astype(F32)
    return hi, value - hi


def norm_rows(hidden):
    center = hidden - jnp.mean(hidden, -1, keepdims=True)
    inverse = lax.rsqrt(jnp.mean(center * center, -1, keepdims=True) + EPS)
    return center * inverse, inverse


def norm_rows_back(grad, normed, inverse, gain):
    scaled = grad * gain
    return inverse * (
        scaled
        - jnp.mean(scaled, -1, keepdims=True)
        - normed * jnp.mean(scaled * normed, -1, keepdims=True)
    )


def project_kernel(x_ref, gain_ref, shift_ref, w_ref, first_ref, q_ref, kv_ref):
    normed, _ = norm_rows(x_ref[...].astype(F32))
    first = (normed * gain_ref[...] + shift_ref[...]).astype(BF16)
    first_ref[...] = first
    out = dot_nn(first, w_ref[...]).astype(BF16)
    q_ref[...] = out[:, : 4 * HD]
    kv_ref[...] = out[:, 4 * HD :]


def project(x, gain, shift, w640):
    rows, width = x.shape
    tile = min(rows, 256)
    row = lambda w: pl.BlockSpec((tile, w), lambda i: (i, 0))
    whole = lambda s: pl.BlockSpec(s, lambda i: (0, 0))
    return pl.pallas_call(
        project_kernel,
        grid=(rows // tile,),
        out_shape=(sds((rows, width), BF16), sds((rows, 4 * HD), BF16), sds((rows, 6 * HD), BF16)),
        in_specs=[row(width), whole((1, width)), whole((1, width)), whole(w640.shape)],
        out_specs=(row(width), row(4 * HD), row(6 * HD)),
        compiler_params=PARAMS,
        name="project",
    )(x, gain, shift, w640)


def gather_kernel(index_ref, blocks_ref, out_ref):
    def step(slot, _):
        out_ref[slot] = blocks_ref[index_ref[slot]]
        return 0

    lax.fori_loop(0, out_ref.shape[0], step, 0)


def gather(blocks, index):
    return call(gather_kernel, sds((index.shape[0],) + blocks.shape[1:], BF16), name="gather")(
        blocks, smem=(index,)
    )


def lead_fwd_kernel(q0_ref, q1_ref, kv_ref, bias_ref, part0_ref, part1_ref):
    batches, per, _ = kv_ref.shape
    rows = 2 * BLOCK
    for m in range(batches):
        tile0 = jnp.concatenate([q0_ref[m, :, : 2 * HD], q1_ref[m, :, : 2 * HD]], 0)
        tile1 = jnp.concatenate([q0_ref[m, :, 2 * HD : 4 * HD], q1_ref[m, :, 2 * HD : 4 * HD]], 0)
        bias = bias_ref[m]
        pair = dot_nt(two_heads(tile0), kv_ref[m, :, : 2 * HD]) + bias
        last = dot_nt(tile1, kv_ref[m, :, 4 * HD :]) + bias
        top_a = jnp.max(pair, -1, keepdims=True)
        top_b = jnp.max(last, -1, keepdims=True)
        exp_a = jnp.exp(pair - top_a)
        exp_b = jnp.exp(last - top_b)
        sum_a = jnp.sum(exp_a, -1, keepdims=True)
        sum_b = jnp.sum(exp_b, -1, keepdims=True)
        out0 = pick_heads(dot_nn(exp_a.astype(BF16), kv_ref[m, :, 2 * HD : 4 * HD]), rows)
        out1 = half(dot_nn(exp_b.astype(BF16), kv_ref[m, :, 4 * HD :]), True)
        stats = lanes_of(
            [top_a[:rows], top_a[rows:], top_b, sum_a[:rows], sum_a[rows:], sum_b], rows
        )
        out1 = out1 + stats
        for end, part_ref in enumerate((part0_ref, part1_ref)):
            at = slice(end * BLOCK, (end + 1) * BLOCK)
            part_ref[m, :, : 2 * HD] = out0[at]
            part_ref[m, :, 2 * HD :] = out1[at]


def merge_kernel(a_ref, b_ref, out_ref):
    for m in range(a_ref.shape[0]):
        st_a = a_ref[m, :, 2 * HD :]
        st_b = b_ref[m, :, 2 * HD :]
        scales_a, scales_b, tops, sums = [], [], [], []
        for h in range(3):
            top_a, top_b = st_a[:, h : h + 1], st_b[:, h : h + 1]
            top = jnp.maximum(top_a, top_b)
            sa, sb = jnp.exp(top_a - top), jnp.exp(top_b - top)
            scales_a.append(sa)
            scales_b.append(sb)
            tops.append(top)
            sums.append(st_a[:, 3 + h : 4 + h] * sa + st_b[:, 3 + h : 4 + h] * sb)
        lane = lax.broadcasted_iota(jnp.int32, (BLOCK, 2 * HD), 1)
        pick = lambda s: jnp.where(lane < HD, s[0], s[1])
        out_ref[m, :, : 2 * HD] = a_ref[m, :, : 2 * HD] * pick(scales_a) + b_ref[
            m, :, : 2 * HD
        ] * pick(scales_b)
        joint = st_a * scales_a[2] + st_b * scales_b[2]
        out_ref[m, :, 2 * HD :] = jnp.where(lane >= HD, joint, lanes_of(tops + sums, BLOCK))


def merge(a, b):
    return call(merge_kernel, sds(a.shape, F32), name="merge")(a, b)


def lead_finish_kernel(part_ref, out_ref, lse_ref):
    for m in range(part_ref.shape[0]):
        st = part_ref[m, :, 2 * HD :]
        lane = lax.broadcasted_iota(jnp.int32, (BLOCK, 2 * HD), 1)
        sums = [st[:, 3 + h : 4 + h] for h in range(3)]
        out_ref[m, :, : 2 * HD] = (
            part_ref[m, :, : 2 * HD] / jnp.where(lane < HD, sums[0], sums[1])
        ).astype(BF16)
        out_ref[m, :, 2 * HD :] = jnp.where(lane >= HD, st / sums[2], 0.0).astype(BF16)
        lse_ref[m] = lanes_of([st[:, h : h + 1] + jnp.log(sums[h]) for h in range(3)], BLOCK)


def fill_ext(ext_ref, kv_ref, low_ref, high_ref, seqs, per):
    for m in range(seqs):
        ext_ref[m, :BLOCK] = low_ref[m]
        ext_ref[m, BLOCK : BLOCK + per] = kv_ref[m]
        ext_ref[m, BLOCK + per :] = high_ref[m]


def fill_listed(listed_ref, ext_ref, lead0_ref, lead1_ref, rand_ref, slot_ref, m, b, block):
    listed_ref[: 3 * BLOCK] = ext_ref[m, pl.ds(pl.multiple_of(b * BLOCK, BLOCK), 3 * BLOCK)]
    listed_ref[3 * BLOCK : 4 * BLOCK] = lead0_ref[m, :, 4 * HD :]
    listed_ref[4 * BLOCK : 5 * BLOCK] = lead1_ref[m, :, 4 * HD :]
    for j in range(RANDS):
        listed_ref[(5 + j) * BLOCK : (6 + j) * BLOCK] = rand_ref[slot_ref[block * RANDS + j]]


def pos_row(meta_ref, m, b, c, chunk, share, seqs):
    token = b * BLOCK + c * chunk
    at = token // share
    j = at ^ meta_ref[0]
    k = ((j & 1) << 1) | (j >> 1)
    return pl.multiple_of(k * (seqs * share) + m * share + (token - at * share), chunk)


def sparse_fwd_kernel(
    first, seqs, per, share, slot_ref, meta_ref, q_ref, kv_ref, low_ref, high_ref, lead0_ref,
    lead1_ref, rand_ref, bias_ref, lead_out_ref, out_ref, lse_ref, ext_ref, listed_ref,
):
    blocks = per // BLOCK
    chunk = min(share, BLOCK)
    fill_ext(ext_ref, kv_ref, low_ref, high_ref, seqs, per)

    def step(i, _):
        m, b = i // blocks, i % blocks
        fill_listed(
            listed_ref, ext_ref, lead0_ref, lead1_ref, rand_ref, slot_ref, m, b, first + i
        )
        bias = bias_ref[i]
        pair = dot_nt(two_heads(q_ref[i, :, : 2 * HD]), listed_ref[:, : 2 * HD]) + bias
        last = dot_nt(q_ref[i, :, 2 * HD :], listed_ref[:, 4 * HD :]) + bias
        top_a = jnp.max(pair, -1, keepdims=True)
        top_b = jnp.max(last, -1, keepdims=True)
        exp_a = jnp.exp(pair - top_a)
        exp_b = jnp.exp(last - top_b)
        sum_a = jnp.sum(exp_a, -1, keepdims=True)
        sum_b = jnp.sum(exp_b, -1, keepdims=True)
        prob_a = (exp_a * (1.0 / sum_a)).astype(BF16)
        prob_b = (exp_b * (1.0 / sum_b)).astype(BF16)
        out0 = pick_heads(dot_nn(prob_a, listed_ref[:, 2 * HD : 4 * HD]), BLOCK).astype(BF16)
        out1 = half(dot_nn(prob_b, listed_ref[:, 4 * HD :]), True).astype(BF16)
        lse_a = top_a + jnp.log(sum_a)
        lse_b = top_b + jnp.log(sum_b)
        lse_ref[i] = lanes_of([lse_a[:BLOCK], lse_a[BLOCK:], lse_b], BLOCK)
        is_lead = ((b == 0) & (meta_ref[1] == 1)) | ((b == blocks - 1) & (meta_ref[2] == 1))
        out0 = jnp.where(is_lead, lead_out_ref[m, :, : 2 * HD], out0)
        out1 = jnp.where(is_lead, lead_out_ref[m, :, 2 * HD :], out1)
        for c in range(BLOCK // chunk):
            row = pos_row(meta_ref, m, b, c, chunk, share, seqs)
            at = slice(c * chunk, (c + 1) * chunk)
            out_ref[pl.ds(row, chunk), : 2 * HD] = out0[at]
            out_ref[pl.ds(row, chunk), 2 * HD :] = out1[at]
        return 0

    lax.fori_loop(0, seqs * blocks, step, 0, unroll=2)


def mid_fwd_kernel(keep_ref, got_ref, x_ref, gain_ref, shift_ref, hidden_ref, act_ref):
    hidden = keep_ref[...] + got_ref[...].astype(F32) + x_ref[...].astype(F32)
    normed, _ = norm_rows(hidden)
    hidden_ref[...] = hidden
    act_ref[...] = (normed * gain_ref[...] + shift_ref[...]).astype(BF16)


def ffn_kernel(act_ref, gu_ref, up_w_ref, up_ref, pre_ref, back_ref):
    pre = dot_nn(act_ref[...], up_w_ref[...])
    phi = 0.5 + 0.5 * lax.erf(pre * (1.0 / math.sqrt(2.0)))
    density = jnp.exp(-0.5 * pre * pre) * (1.0 / math.sqrt(2.0 * math.pi))
    up_ref[...] = (pre * phi).astype(BF16)
    grad_pre = (gu_ref[...] * (phi + pre * density)).astype(BF16)
    pre_ref[...] = grad_pre
    back_ref[...] = dot_nt(grad_pre, up_w_ref[...]).astype(BF16)


def ffn(act, gu, w_up):
    rows, width = act.shape
    hidden = w_up.shape[1]
    tile = 128
    row = lambda w: pl.BlockSpec((tile, w), lambda i: (i, 0))
    return pl.pallas_call(
        ffn_kernel,
        grid=(rows // tile,),
        out_shape=(sds((rows, hidden), BF16), sds((rows, hidden), BF16), sds((rows, width), BF16)),
        in_specs=[row(width), row(hidden), pl.BlockSpec((width, hidden), lambda i: (0, 0))],
        out_specs=(row(hidden), row(hidden), row(width)),
        compiler_params=PARAMS,
        name="ffn",
    )(act, gu, w_up)


def mid_bwd_kernel(keep_ref, got_ref, hidden_ref, out_grad_ref, gain_ref, total_ref, low_ref, sums_ref):
    grad = keep_ref[...] + got_ref[...].astype(F32)
    normed, inverse = norm_rows(hidden_ref[...])
    total = out_grad_ref[...].astype(F32) + norm_rows_back(grad, normed, inverse, gain_ref[...])
    total_ref[...] = total
    low_ref[...] = total.astype(BF16)
    sums_ref[0:1] = jnp.sum(grad * normed, 0, keepdims=True)
    sums_ref[1:2] = jnp.sum(grad, 0, keepdims=True)


def end_kernel(keep_ref, got_ref, x_ref, total_ref, gain_ref, out_ref):
    grad = keep_ref[...] + got_ref[...].astype(F32)
    normed, inverse = norm_rows(x_ref[...].astype(F32))
    out_ref[...] = total_ref[...] + norm_rows_back(grad, normed, inverse, gain_ref[...])


def heads_grad_kernel(
    groups, seqs, per, share, index_ref, meta_ref, *refs,
):
    mixed_refs, outs_refs = refs[:groups], refs[groups : 2 * groups]
    lse_ref, lead_lse_ref, grads_ref, sent_ref, lead_ref, lead_grad = refs[2 * groups :]
    blocks = per // BLOCK
    chunk = min(share, BLOCK)
    for g in range(groups):

        def step(i, _, g=g):
            m, b = i // blocks, i % blocks
            at = g * seqs * blocks + i
            gsum, dsum = [], []
            for c in range(BLOCK // chunk):
                row = pos_row(meta_ref, m, b, c, chunk, share, seqs)
                gsum.append(mixed_refs[g][pl.ds(row, chunk)])
                dsum.append(outs_refs[g][pl.ds(row, chunk)])
            grad = gsum[0] if len(gsum) == 1 else jnp.concatenate(gsum, 0)
            outs = dsum[0] if len(dsum) == 1 else jnp.concatenate(dsum, 0)
            prod = grad.astype(F32) * outs.astype(F32)
            first, second = prod[:, : 2 * HD], prod[:, 2 * HD :]
            deltas = [
                jnp.sum(half(first, False), -1, keepdims=True),
                jnp.sum(half(first, True), -1, keepdims=True),
                jnp.sum(half(second, True), -1, keepdims=True),
            ]
            d_hi, d_lo = zip(*(hi_lo(d) for d in deltas))
            is_lead = ((b == 0) & (meta_ref[1] == 1)) | ((b == blocks - 1) & (meta_ref[2] == 1))

            def stats(lse):
                l_hi, l_lo = zip(*(hi_lo(lse[:, h : h + 1]) for h in range(3)))
                return l_hi + l_lo

            low = half(grad[:, 2 * HD :], True).astype(F32)
            zero = jnp.zeros_like(deltas[0])

            @pl.when(is_lead)
            def _():
                lead_ref[g * seqs + m, :, : 2 * HD] = grad[:, : 2 * HD]
                lead_ref[g * seqs + m, :, 2 * HD :] = (
                    low + lanes_of(stats(lead_lse_ref[g * seqs + m]) + d_hi + d_lo, BLOCK)
                ).astype(BF16)

            scale = jnp.where(is_lead, 0.0, 1.0)
            grads_ref[at, :, : 2 * HD] = (grad[:, : 2 * HD].astype(F32) * scale).astype(BF16)
            grads_ref[at, :, 2 * HD :] = (
                low * scale
                + lanes_of(
                    stats(lse_ref[at]) + tuple(d * scale for d in d_hi) + tuple(d * scale for d in d_lo),
                    BLOCK,
                )
            ).astype(BF16)
            return 0

        lax.fori_loop(0, seqs * blocks, step, 0)

    def send(slot, _):
        sent_ref[slot] = grads_ref[index_ref[slot]]
        return 0

    lax.fori_loop(0, sent_ref.shape[0], send, 0)


def row_stats(tile):
    st = tile.astype(F32)
    lse = [st[:, h : h + 1] + st[:, 3 + h : 4 + h] for h in range(3)]
    delta = [st[:, 6 + h : 7 + h] + st[:, 9 + h : 10 + h] for h in range(3)]
    return lse, delta


def sparse_bwd_kernel(
    batches, per, slot_ref, q_ref, kv_ref, low_ref, high_ref, lead0_ref, lead1_ref, rand_ref,
    bias_ref, grads_ref, dq_ref, dkv_ref, ret_low_ref, ret_high_ref, dlead0_ref, dlead1_ref,
    ext_ref, listed_ref, dext_ref, dlead_ref,
):
    blocks = per // BLOCK
    fill_ext(ext_ref, kv_ref, low_ref, high_ref, batches, per)
    dext_ref[...] = jnp.zeros_like(dext_ref)
    dlead_ref[...] = jnp.zeros_like(dlead_ref)

    def step(i, _):
        m, b = i // blocks, i % blocks
        fill_listed(listed_ref, ext_ref, lead0_ref, lead1_ref, rand_ref, slot_ref, m, b, i)
        bias = bias_ref[i]
        tile1 = grads_ref[i, :, 2 * HD :]
        lse, delta = row_stats(tile1)
        q_a, q_b = two_heads(q_ref[i, :, : 2 * HD]), q_ref[i, :, 2 * HD :]
        do_a, do_b = two_heads(grads_ref[i, :, : 2 * HD]), half(tile1, True)
        prob_a = jnp.exp(
            dot_nt(q_a, listed_ref[:, : 2 * HD]) + bias - jnp.concatenate(lse[:2], 0)
        )
        prob_b = jnp.exp(dot_nt(q_b, listed_ref[:, 4 * HD :]) + bias - lse[2])
        ds_a = prob_a * (
            dot_nt(do_a, listed_ref[:, 2 * HD : 4 * HD]) - jnp.concatenate(delta[:2], 0)
        )
        ds_b = prob_b * (dot_nt(do_b, listed_ref[:, 4 * HD :]) - delta[2])
        ds_a, ds_b = ds_a.astype(BF16), ds_b.astype(BF16)
        dq_ref[i, :, : 2 * HD] = pick_heads(dot_nn(ds_a, listed_ref[:, : 2 * HD]), BLOCK)
        dq_ref[i, :, 2 * HD :] = half(dot_nn(ds_b, listed_ref[:, 4 * HD :]), False)
        near = 6 * BLOCK
        prob_a, prob_b = prob_a[:, :near].astype(BF16), prob_b[:, :near].astype(BF16)
        dkv = jnp.concatenate(
            [
                dot_tn(ds_a[:, :near], q_a),
                dot_tn(prob_a, do_a),
                dot_tn(ds_b[:, :near], q_b) + dot_tn(prob_b, do_b),
            ],
            1,
        )
        dext_ref[m, pl.ds(pl.multiple_of(b * BLOCK, BLOCK), 3 * BLOCK)] += dkv[: 3 * BLOCK]
        dlead_ref[m] += dkv[3 * BLOCK : 5 * BLOCK]
        return 0

    lax.fori_loop(0, batches * blocks, step, 0, unroll=2)
    for m in range(batches):
        ret_low_ref[m] = dext_ref[m, :BLOCK].astype(BF16)
        dkv_ref[m] = dext_ref[m, BLOCK : BLOCK + per]
        ret_high_ref[m] = dext_ref[m, BLOCK + per :].astype(BF16)
        dlead0_ref[m] = dlead_ref[m, :BLOCK]
        dlead1_ref[m] = dlead_ref[m, BLOCK:]


def lead_bwd_kernel(q0_ref, q1_ref, do0_ref, do1_ref, kv_ref, bias_ref, dkv_ref, dq0_ref, dq1_ref):
    rows = 2 * BLOCK
    for m in range(kv_ref.shape[0]):
        both = lambda a, b, lo, hi: jnp.concatenate([a[m, :, lo:hi], b[m, :, lo:hi]], 0)
        tile1 = both(do0_ref, do1_ref, 2 * HD, 4 * HD)
        lse, delta = row_stats(tile1)
        q_a = two_heads(both(q0_ref, q1_ref, 0, 2 * HD))
        q_b = both(q0_ref, q1_ref, 2 * HD, 4 * HD)
        do_a, do_b = two_heads(both(do0_ref, do1_ref, 0, 2 * HD)), half(tile1, True)
        k_a, v_a, kv_b = kv_ref[m, :, : 2 * HD], kv_ref[m, :, 2 * HD : 4 * HD], kv_ref[m, :, 4 * HD :]
        bias = bias_ref[m]
        prob_a = jnp.exp(dot_nt(q_a, k_a) + bias - jnp.concatenate(lse[:2], 0))
        prob_b = jnp.exp(dot_nt(q_b, kv_b) + bias - lse[2])
        ds_a = (prob_a * (dot_nt(do_a, v_a) - jnp.concatenate(delta[:2], 0))).astype(BF16)
        ds_b = (prob_b * (dot_nt(do_b, kv_b) - delta[2])).astype(BF16)
        dq_a = pick_heads(dot_nn(ds_a, k_a), rows)
        dq_b = half(dot_nn(ds_b, kv_b), False)
        for end, dq_ref in enumerate((dq0_ref, dq1_ref)):
            at = slice(end * BLOCK, (end + 1) * BLOCK)
            dq_ref[m, :, : 2 * HD] = dq_a[at]
            dq_ref[m, :, 2 * HD :] = dq_b[at]
        dkv_ref[m, :, : 2 * HD] = dot_tn(ds_a, q_a)
        dkv_ref[m, :, 2 * HD : 4 * HD] = dot_tn(prob_a.astype(BF16), do_a)
        dkv_ref[m, :, 4 * HD :] = dot_tn(ds_b, q_b) + dot_tn(prob_b.astype(BF16), do_b)


def tail_kernel(
    groups, seqs, per, share, index_ref, valid_ref, meta_ref, q_got_ref, do_got_ref, kv_ref,
    column_ref, dq_ref, dkv_ref, dkv_lead_ref, ret_low_ref, ret_high_ref, ends_ref, first_ref, x_ref, w_ref,
    gw_ref, back_ref, sums_ref, acc_ref, gqkv_ref,
):
    blocks = per // BLOCK
    chunk = min(share, BLOCK)
    total = groups * seqs * blocks
    head, tail = meta_ref[1], meta_ref[2]

    def start(i, _):
        m, b = i // blocks, i % blocks
        acc_ref[i] = dkv_ref[i] + dkv_lead_ref[i]

        @pl.when(b == 0)
        def _():
            acc_ref[i] += ret_low_ref[m].astype(F32)

        @pl.when(b == blocks - 1)
        def _():
            acc_ref[i] += ret_high_ref[m].astype(F32)

        @pl.when(((b == 0) & (head == 1)) | ((b == blocks - 1) & (tail == 1)))
        def _():
            acc_ref[i] += ends_ref[m, :, 4 * HD :].astype(F32)

        return 0

    lax.fori_loop(0, total, start, 0)

    def slot(c, _):
        @pl.when(valid_ref[c] == 1)
        def _():
            at = index_ref[c]
            kv = kv_ref[at]
            tile1 = do_got_ref[c, :, 2 * HD :]
            stats = jnp.transpose(tile1.astype(F32))
            lse = [stats[h : h + 1] + stats[3 + h : 4 + h] for h in range(3)]
            delta = [stats[6 + h : 7 + h] + stats[9 + h : 10 + h] for h in range(3)]
            q_a, q_b = two_heads(q_got_ref[c, :, : 2 * HD]), q_got_ref[c, :, 2 * HD :]
            do_a, do_b = two_heads(do_got_ref[c, :, : 2 * HD]), half(tile1, True)
            bias = column_ref[at]
            prob_a = jnp.exp(
                dot_nt(kv[:, : 2 * HD], q_a) + bias - jnp.concatenate(lse[:2], 1)
            )
            prob_b = jnp.exp(dot_nt(kv[:, 4 * HD :], q_b) + bias[:, :BLOCK] - lse[2])
            ds_a = prob_a * (
                dot_nt(kv[:, 2 * HD : 4 * HD], do_a) - jnp.concatenate(delta[:2], 1)
            )
            ds_b = prob_b * (dot_nt(kv[:, 4 * HD :], do_b) - delta[2])
            acc_ref[at] += jnp.concatenate(
                [
                    dot_nn(ds_a.astype(BF16), q_a),
                    dot_nn(prob_a.astype(BF16), do_a),
                    dot_nn(ds_b.astype(BF16), q_b) + dot_nn(prob_b.astype(BF16), do_b),
                ],
                1,
            )

        return 0

    lax.fori_loop(0, q_got_ref.shape[0], slot, 0, unroll=2)

    def finish(i, _):
        m, b = i // blocks, i % blocks
        dq = dq_ref[i]
        is_end = ((b == 0) & (head == 1)) | ((b == blocks - 1) & (tail == 1))
        dq = dq + jnp.where(is_end, ends_ref[m, :, : 4 * HD].astype(F32), 0.0)
        rows = pl.ds(pl.multiple_of(i * BLOCK, BLOCK), BLOCK)
        gqkv_ref[rows, : 4 * HD] = dq.astype(BF16)
        gqkv_ref[rows, 4 * HD :] = acc_ref[i].astype(BF16)
        return 0

    lax.fori_loop(0, total, finish, 0)
    sums_ref[...] = jnp.zeros_like(sums_ref)
    tile = 128 if per % 128 == 0 else BLOCK

    def project_back(i, _):
        rows = pl.ds(pl.multiple_of(i * tile, tile), tile)
        back = dot_nt(gqkv_ref[rows], w_ref[...])
        normed, _ = norm_rows(x_ref[rows].astype(F32))
        sums_ref[0:1] += jnp.sum(back * normed, 0, keepdims=True)
        sums_ref[1:2] += jnp.sum(back, 0, keepdims=True)
        low = back.astype(BF16)
        m, inside = i // (per // tile), (i % (per // tile)) * tile
        g, m = m // seqs, m % seqs
        for c in range(tile // chunk):
            token = inside + c * chunk
            at = token // share
            j = at ^ meta_ref[0]
            k = ((j & 1) << 1) | (j >> 1)
            row = pl.multiple_of(k * (seqs * share) + m * share + (token - at * share), chunk)
            back_ref[g, pl.ds(row, chunk)] = low[c * chunk : (c + 1) * chunk]
        return 0

    lax.fori_loop(0, total * BLOCK // tile, project_back, 0)
    gw_ref[...] = dot_tn(first_ref[...], gqkv_ref[...]).astype(BF16)


def swap_tp(value, bit):
    return lax.ppermute(value, "tp", [(i, i ^ bit) for i in range(lax.axis_size("tp"))])


def scatter_tp(part):
    rows = part.shape[0] // 2
    got = swap_tp(part[rows:], 1)
    both = part[:rows].astype(F32) + got.astype(F32)
    piece = rows // 2
    return both[:piece], swap_tp(both[piece:].astype(BF16), 2)


def gather_tp(piece):
    near = jnp.concatenate([piece, swap_tp(piece, 2)], 0)
    return jnp.concatenate([near, swap_tp(near, 1)], 0)


def tree_out(own, myself, devices):
    held = own
    bit = 1
    while bit < devices // 2:
        pairs = [(i, i + bit) for i in range(bit)]
        pairs += [(devices - 1 - a, devices - 1 - b) for a, b in pairs]
        got = lax.ppermute(held, "seq", pairs)
        lower = (myself >= bit) & (myself < 2 * bit)
        rest = devices - 1 - myself
        upper = (rest >= bit) & (rest < 2 * bit)
        held = jnp.where(lower | upper, got, held)
        bit *= 2
    other = lax.ppermute(held, "seq", [(i, i ^ bit) for i in range(devices)])
    low = myself < devices // 2
    return jnp.where(low, held, other), jnp.where(low, other, held)


def tree_in(for_first, for_last, myself, devices, join):
    low = myself < devices // 2
    bit = devices // 2
    mine = jnp.where(low, for_first, for_last)
    given = jnp.where(low, for_last, for_first)
    mine = join(mine, lax.ppermute(given, "seq", [(i, i ^ bit) for i in range(devices)]))
    while bit > 1:
        bit //= 2
        pairs = [(i + bit, i) for i in range(bit)]
        pairs += [(devices - 1 - a, devices - 1 - b) for a, b in pairs]
        mine = join(mine, lax.ppermute(mine, "seq", pairs))
    return mine


def to_owners(slots):
    return lax.all_to_all(slots, "seq", split_axis=0, concat_axis=0, tiled=True)


def per_device(
    layer_input,
    out_grad,
    norm1_gain,
    norm1_shift,
    w_qkv,
    w_out,
    norm2_gain,
    norm2_shift,
    w_up,
    w_down,
    key_keep,
    rand_blocks,
):
    batches, per, width = layer_input.shape
    local = w_qkv.shape[2]
    devices = lax.axis_size("seq")
    myself = lax.axis_index("seq")
    tp_count = lax.axis_size("tp")
    tp_place = lax.axis_index("tp")
    assert local == 3 * HD and tp_count == 4 and devices % 2 == 0
    share = per // tp_count
    bd = per // BLOCK
    total = batches * bd
    blocks_all = bd * devices
    groups = 2 if batches % 2 == 0 else 1
    seqs = batches // groups
    piece = seqs * share
    refs = total * RANDS
    slots_per = max(1, -(-refs // devices))
    slots = devices * slots_per
    i32 = jnp.int32
    row = lambda v: v.reshape(1, -1)
    gain1, shift1, gain2, shift2 = map(row, (norm1_gain, norm1_shift, norm2_gain, norm2_shift))
    meta = jnp.stack(
        [tp_place, (myself == 0).astype(i32), (myself == devices - 1).astype(i32)]
    ).astype(i32)

    blank = jnp.zeros((width, HD), BF16)
    wq, wk, wv = (w_qkv[:, c] for c in range(3))
    scale = 1.0 / math.sqrt(HD)
    w640 = jnp.concatenate(
        [wq * jnp.asarray(scale, BF16), blank, wk[:, : 2 * HD], wv[:, : 2 * HD], wk[:, 2 * HD :], wv[:, 2 * HD :]], 1
    )
    wo256 = jnp.concatenate([w_out[:, : 2 * HD], blank, w_out[:, 2 * HD :]], 1)

    x_rows = layer_input.reshape(batches * per, width)
    first, q, kv = project(x_rows, gain1, shift1, w640)
    q_blocks = q.reshape(total, BLOCK, 4 * HD)
    kv_blocks = kv.reshape(total, BLOCK, 6 * HD)
    q_seqs = q.reshape(batches, per, 4 * HD)
    kv_seqs = kv.reshape(batches, per, 6 * HD)

    table = (
        rand_blocks.reshape(batches, devices, bd, RANDS).transpose(1, 0, 2, 3).reshape(devices, refs)
    )
    owners = table // bd
    source = (jnp.arange(refs, dtype=i32) // (bd * RANDS))[None] * bd + table - owners * bd
    order = jnp.arange(refs, dtype=i32)
    earlier = order[None, :] < order[:, None]
    rank = jnp.sum(((owners[:, :, None] == owners[:, None, :]) & earlier[None]).astype(i32), -1)
    places = jnp.arange(slots_per, dtype=i32)
    asked = (owners == myself)[:, None, :] & (rank[:, None, :] == places[None, :, None])
    source_of = jnp.sum(jnp.where(asked, source[:, None, :], 0), -1).reshape(slots)
    valid = jnp.sum(asked.astype(i32), -1).reshape(slots)
    my_owner = lax.dynamic_index_in_dim(owners, myself, 0, False)
    my_rank = lax.dynamic_index_in_dim(rank, myself, 0, False)
    slot_of = my_owner * slots_per + my_rank
    query_of = jnp.sum(
        jnp.where(
            slot_of[None, :] == jnp.arange(slots, dtype=i32)[:, None], (order // RANDS)[None, :], 0
        ),
        -1,
    )

    rand_kv = to_owners(gather(kv_blocks, source_of))
    ends = jnp.where(
        myself < devices // 2,
        jnp.concatenate([q_seqs[:, :BLOCK], kv_seqs[:, :BLOCK]], 2),
        jnp.concatenate([q_seqs[:, per - BLOCK :], kv_seqs[:, per - BLOCK :]], 2),
    )
    lead0, lead1 = tree_out(ends, myself, devices)
    up = [(i, i + 1) for i in range(devices - 1)]
    down = [(b, a) for a, b in up]
    low = lax.ppermute(kv_seqs[:, per - BLOCK :], "seq", up)
    high = lax.ppermute(kv_seqs[:, :BLOCK], "seq", down)

    keep = key_keep.reshape(batches, blocks_all, BLOCK)
    padded = jnp.pad(keep, ((0, 0), (1, 1), (0, 0)))
    window = lax.dynamic_slice_in_dim(padded, myself * bd, bd + 2, 1)
    mine = lax.dynamic_index_in_dim(table, myself, 0, False).reshape(batches, bd * RANDS)
    hot = (mine[:, :, None] == jnp.arange(blocks_all, dtype=i32)).astype(BF16)
    rand_keep = jnp.einsum("mjn,mnb->mjb", hot, keep.astype(BF16)).astype(i32)
    listed_keep = jnp.concatenate(
        [window[:, i : i + bd] for i in range(3)]
        + [
            jnp.broadcast_to(keep[:, :1], (batches, bd, BLOCK)),
            jnp.broadcast_to(keep[:, blocks_all - 1 :], (batches, bd, BLOCK)),
            rand_keep.reshape(batches, bd, RANDS * BLOCK),
        ],
        2,
    )
    bias = jnp.where(listed_keep > 0, 0.0, NEG).astype(F32).reshape(total, 1, 8 * BLOCK)
    own_keep = window[:, 1 : bd + 1]
    own_bias = jnp.where(own_keep > 0, 0.0, NEG).astype(F32)
    seq_bias = own_bias.reshape(batches, 1, per)
    column_bias = jnp.broadcast_to(own_bias.reshape(total, BLOCK, 1), (total, BLOCK, 2 * HD))

    part = sds((batches, BLOCK, 4 * HD), F32)
    part0, part1 = call(lead_fwd_kernel, (part, part), name="lead_fwd")(
        lead0, lead1, kv_seqs, seq_bias
    )
    lead_part = tree_in(part0, part1, myself, devices, merge)
    lead_out, lead_lse = call(
        lead_finish_kernel, (sds(part.shape, BF16), sds((batches, BLOCK, 2 * HD), F32)), name="lead_finish"
    )(lead_part)

    def own_share(value, g):
        return lax.dynamic_slice(
            value, (g * seqs, tp_place * share, 0), (seqs, share, width)
        ).reshape(piece, width)

    def in_pos_order(value, g):
        return jnp.concatenate(
            [
                lax.dynamic_slice(
                    value, (g * seqs, (tp_place ^ SWAP[k]) * share, 0), (seqs, share, width)
                ).reshape(piece, width)
                for k in range(4)
            ],
            0,
        )

    x_share = [own_share(layer_input, g) for g in range(groups)]
    og_share = [own_share(out_grad, g) for g in range(groups)]
    og_pos = [in_pos_order(out_grad, g) for g in range(groups)]
    grad_up = [dot_nn(og_pos[g], w_down) for g in range(groups)]

    mixed, lse = [], []
    for g in range(groups):
        seq_at = slice(g * seqs, (g + 1) * seqs)
        at = slice(g * seqs * bd, (g + 1) * seqs * bd)
        out, stat = call(
            partial(sparse_fwd_kernel, g * seqs * bd, seqs, per, share),
            (sds((4 * piece, 4 * HD), BF16), sds((seqs * bd, BLOCK, 2 * HD), F32)),
            (
                pltpu.VMEM((seqs, per + 2 * BLOCK, 6 * HD), BF16),
                pltpu.VMEM((8 * BLOCK, 6 * HD), BF16),
            ),
            name="sparse_fwd",
        )(
            q_blocks[at], kv_seqs[seq_at], low[seq_at], high[seq_at], lead0[seq_at], lead1[seq_at],
            rand_kv, bias[at], lead_out[seq_at], smem=(slot_of, meta),
        )
        mixed.append(out)
        lse.append(stat)
    lse = jnp.concatenate(lse, 0)

    q_slots, _ = lax.optimization_barrier((gather(q_blocks, query_of), rand_kv))
    rand_q = to_owners(q_slots)

    hidden, act, ups, pres, back = [], [], [], [], []
    for g in range(groups):
        kept, got = scatter_tp(dot_nt(mixed[g], wo256).astype(BF16))
        h, a = call(
            mid_fwd_kernel, (sds((piece, width), F32), sds((piece, width), BF16)), name="mid_fwd"
        )(kept, got, x_share[g], gain2, shift2)
        hidden.append(h)
        act.append(gather_tp(a))
    for g in range(groups):
        u, p, b = ffn(act[g], grad_up[g], w_up)
        ups.append(u)
        pres.append(p)
        back.append(b)

    total_grad, sums2, mixed_grad, attn_grad = [], [], [], []
    for g in range(groups):
        kept, got = scatter_tp(back[g])
        t, a, s = call(
            mid_bwd_kernel,
            (sds((piece, width), F32), sds((piece, width), BF16), sds((2, width), F32)),
            name="mid_bwd",
        )(kept, got, hidden[g], og_share[g], gain2)
        total_grad.append(t)
        sums2.append(s)
        attn_grad.append(gather_tp(a))
        mixed_grad.append(dot_nn(attn_grad[g], wo256).astype(BF16))

    outputs = []
    for g in range(groups):
        kept, got = scatter_tp(dot_nt(ups[g], w_down).astype(BF16))
        outputs.append((hidden[g] + kept + got.astype(F32)).reshape(seqs, share, width))
    layer_output = jnp.concatenate(outputs, 0)
    every = lambda parts: jnp.concatenate(parts, 0)
    gw_down = dot_tn(every(og_pos), every(ups))
    gw_up = dot_tn(every(act), every(pres))
    gw_out = dot_tn(every(attn_grad), every(mixed))
    gw_out = jnp.concatenate([gw_out[:, : 2 * HD], gw_out[:, 3 * HD :]], 1)

    grads, sent, lead_grad = call(
        partial(heads_grad_kernel, groups, seqs, per, share),
        (
            sds((total, BLOCK, 4 * HD), BF16),
            sds((slots, BLOCK, 4 * HD), BF16),
            sds((batches, BLOCK, 4 * HD), BF16),
        ),
        (pltpu.VMEM((8, 2 * HD), F32),),
        name="heads_grad",
    )(*mixed_grad, *mixed, lse, lead_lse, smem=(query_of, meta))
    rand_do = to_owners(sent)
    lead_do0, lead_do1 = tree_out(lead_grad, myself, devices)
    end = sds((batches, BLOCK, 6 * HD), BF16)
    dq, dkv, ret_low, ret_high, dlead0, dlead1 = call(
        partial(sparse_bwd_kernel, batches, per),
        (
            sds((total, BLOCK, 4 * HD), F32),
            sds((batches, per, 6 * HD), F32),
            end,
            end,
            sds(end.shape, F32),
            sds(end.shape, F32),
        ),
        (
            pltpu.VMEM((batches, per + 2 * BLOCK, 6 * HD), BF16),
            pltpu.VMEM((8 * BLOCK, 6 * HD), BF16),
            pltpu.VMEM((batches, per + 2 * BLOCK, 6 * HD), F32),
            pltpu.VMEM((batches, 2 * BLOCK, 6 * HD), F32),
        ),
        name="sparse_bwd",
    )(
        q_blocks, kv_seqs, low, high, lead0, lead1, rand_kv, bias, grads, smem=(slot_of,)
    )
    from_low = lax.ppermute(ret_high, "seq", up)
    from_high = lax.ppermute(ret_low, "seq", down)
    dkv_lead, dq0, dq1 = call(
        lead_bwd_kernel, (sds((batches, per, 6 * HD), F32), part, part), name="lead_bwd"
    )(lead0, lead1, lead_do0, lead_do1, kv_seqs, seq_bias)
    add = lambda a, b: (a.astype(F32) + b.astype(F32)).astype(BF16)
    ends_grad = tree_in(
        jnp.concatenate([dq0, dlead0], 2).astype(BF16),
        jnp.concatenate([dq1, dlead1], 2).astype(BF16),
        myself,
        devices,
        add,
    )
    gw_qkv, first_back, sums1 = call(
        partial(tail_kernel, groups, seqs, per, share),
        (sds((width, 10 * HD), BF16), sds((groups, 4 * piece, width), BF16), sds((2, width), F32)),
        (pltpu.VMEM((total, BLOCK, 6 * HD), F32), pltpu.VMEM((total * BLOCK, 10 * HD), BF16)),
        name="tail",
    )(
        rand_q, rand_do, kv_blocks, column_bias, dq, dkv.reshape(total, BLOCK, 6 * HD),
        dkv_lead.reshape(total, BLOCK, 6 * HD), from_low, from_high, ends_grad, first, x_rows, w640,
        smem=(source_of, valid, meta),
    )

    input_parts = []
    for g in range(groups):
        kept, got = scatter_tp(first_back[g])
        input_parts.append(
            call(end_kernel, sds((piece, width), F32), name="end")(
                kept, got, x_share[g], total_grad[g], gain1
            ).reshape(seqs, share, width)
        )
    input_grad = jnp.concatenate(input_parts, 0)

    ff = lax.psum_scatter(
        jnp.concatenate([gw_down, gw_up, gw_out], 1).astype(BF16), "seq", scatter_dimension=0, tiled=True
    ).astype(F32)
    hidden_here = w_up.shape[1]
    g_down, g_up, g_out = ff[:, :hidden_here], ff[:, hidden_here : 2 * hidden_here], ff[:, 2 * hidden_here :]
    rows = width // devices
    gq = to_owners(gw_qkv).reshape(devices, rows, 10 * HD).astype(F32).sum(0)
    g_qkv = jnp.stack(
        [
            gq[:, : 3 * HD] * scale,
            jnp.concatenate([gq[:, 4 * HD : 6 * HD], gq[:, 8 * HD : 9 * HD]], 1),
            jnp.concatenate([gq[:, 6 * HD : 8 * HD], gq[:, 9 * HD :]], 1),
        ],
        1,
    )
    norms = jnp.concatenate([sums1, sum(sums2)], 0).reshape(4, devices, 1, rows)
    norms = jnp.broadcast_to(norms.transpose(1, 2, 0, 3), (devices, tp_count, 4, rows))
    norms = lax.all_to_all(
        norms.reshape(devices * tp_count, 4, rows), ("seq", "tp"), split_axis=0, concat_axis=0, tiled=True
    ).sum(0)
    return (
        layer_output, input_grad, g_qkv, g_out, g_up, g_down, norms[0], norms[1], norms[2], norms[3],
    )


def solution(mesh):
    return jax.shard_map(
        per_device,
        mesh=mesh,
        in_specs=(
            P(None, "seq", None),
            P(None, "seq", None),
            P(),
            P(),
            P(None, None, "tp"),
            P(None, "tp"),
            P(),
            P(),
            P(None, "tp"),
            P(None, "tp"),
            P(),
            P(),
        ),
        out_specs=(
            P(None, ("seq", "tp"), None),
            P(None, ("seq", "tp"), None),
            P("seq", None, "tp"),
            P("seq", "tp"),
            P("seq", "tp"),
            P("seq", "tp"),
            P("seq"),
            P("seq"),
            P("seq"),
            P("seq"),
        ),
        check_vma=False,
    )
```

time: 1240 us -> 450 us (0.36)
  waiting for transfers between devices: 664 us -> 89.1 us
  local copies, waits for them, and re-layouts: 228 us -> 90 us
  blocking collectives: 122 us -> 0 us
  Pallas kernels: 0 us -> 111 us
  matrix products: 87.1 us -> 22 us
  starting transfers between devices: 26.2 us -> 84 us
  other arithmetic: 84.1 us -> 34.9 us
    psum x6 -> x0, waiting for transfers between devices: 431 us -> none  [the longest x3 224 us: head_total(): return lax.psum(value, 'tp')]
    reduce_scatter x3 -> x0, waiting for transfers between devices: 161 us -> none  [the longest x1 72.1 us: per_device(): lax.psum_scatter(grad_w_up, 'seq', scatter_dimension=0, tiled=True)]
    pallas_call x0 -> x22, Pallas kernels: none -> 111 us  [the longest x19 94.3 us: run(): pl.pallas_call(body, out_shape=outs, in_specs=specs, out_specs=jax.tree.m...]
    ppermute x4 -> x40, waiting for transfers between devices: 0.01 us -> 85.1 us  [the longest x4 24.6 us: tree_out(): got = lax.ppermute(held, 'seq', pairs)]
    all_gather x3 -> x0, blocking collectives: 84.5 us -> none  [combined_all(): lax.all_gather(a.astype(kind), axis)]
    unnamed x11 -> x2, waiting for transfers between devices: 72.3 us -> 0.02 us
    dot_general x30 -> x12, matrix products: 87.1 us -> 22 us  [the longest x3 8.44 us: dot_tn(): lax.dot_general(a, b, (((0,), (0,)), ((), ())), preferred_element_type=F32)]
    slice x17 -> x48, local copies, waits for them, and re-layouts: 90.6 us -> 27.7 us  [the longest x14 5.49 us: scatter_tp(): return (both[:piece], swap_tp(both[piece:].astype(BF16), 2))]
  transfers between devices with their start and end apart: 16 -> 46, of which waited for: 10 -> 19; matrix products, arithmetic and copies ran while one was open for 14% -> 28% of each run, Pallas kernels for 0% -> 22%
where the time goes in v1:
time: 450 us; the launch traced here: 447 us
  Pallas kernels  111 us (25%)
  local copies, waits for them, and re-layouts  90 us (20%)
  waiting for transfers between devices  89.1 us (20%)
  starting transfers between devices  84 us (19%)
  other arithmetic  34.9 us (8%)
  matrix products  22 us (5%)
  between operations  15.3 us (3%)
    pallas_call x19, Pallas kernels, run(): pl.pallas_call(body, out_shape=outs, in_specs=specs, out_specs=jax.tree.m...  94.3 us
    unnamed x169, local copies, waits for them, and re-layouts  35.1 us
    ppermute x4, waiting for transfers between devices, tree_out(): got = lax.ppermute(held, 'seq', pairs)  24.6 us
    all_to_all x4, starting transfers between devices, to_owners(): return lax.all_to_all(slots, 'seq', split_axis=0, concat_axis=0, tiled=True)  17.4 us
    ppermute x24, waiting for transfers between devices, swap_tp(): lax.ppermute(value, 'tp', [(i, i ^ bit) for i in range(lax.axis_size('tp'...  17.4 us
    ppermute x4, starting transfers between devices, tree_out(): got = lax.ppermute(held, 'seq', pairs)  16.7 us
    ppermute x24, starting transfers between devices, swap_tp(): lax.ppermute(value, 'tp', [(i, i ^ bit) for i in range(lax.axis_size('tp'...  15.2 us
    ppermute x2, waiting for transfers between devices, tree_out(): other = lax.ppermute(held, 'seq', [(i, i ^ bit) for i in range(devices)])  13.9 us
  transfers between devices with their start and end apart: 46, of which 19 were waited for; matrix products, arithmetic and copies ran while one was open for 28% of the time, Pallas kernels for 22%

profile of v1, /device:TPU:0, one launch (start us, length us, event | category | flops | bytes accessed | tf_op | source)
XLA Modules:
  0.0 446.7 jit_solution(11320760853034570711)
XLA Ops:
  12.4 5.3 %project.1 = (bf16[1024,768]{1,0:T(8,128)(2,1)}, bf16[1024,256]{1,0:T(8,128)(2,1)}, bf16[1024,384]{1,0:T(8,128)(2,1)}) custom-call(bf16[1024,768]{1,0:T(8,128)(2,1)} %bitcast.122, f32[1,768]{1,0:T(1,128)} %reshape.372.gain_ref, f32[1,768]{1,0:T(1,128)} %reshape.373.shift_ref, bf16[768,640]{1,0:T(8,128)(2,1)} %concatenate.121.w_ref), custom_call_target="tpu_custom_call" | custom-call | tf_op jit(solution)/shard_map/project/pallas_call | solution.py:114
  20.7 6.1 %collective-permute-start = (bf16[2,64,384]{2,1,0:T(8,128)(2,1)}, bf16[2,64,384]{2,1,0:T(8,128)(2,1)}, u32[]{:S(2)}, u32[]{:S(2)}) collective-permute-start(bf16[2,64,384]{2,1,0:T(8,128)(2,1)} %get-tuple-element.188), channel_id=1, source_target_pairs={{0,4},{4,8},{8,12},{12,16},{16,20},{20,24},{24,28},{1,5},{5,9},{9,... | collective-permute-start | bytes 294920 | tf_op jit(solution)/shard_map/ppermute | solution.py:701
  29.3 4.8 %collective-permute-start.2 = (bf16[2,64,640]{2,1,0:T(8,128)(2,1)}, bf16[2,64,640]{2,1,0:T(8,128)(2,1)}, u32[]{:S(2)}, u32[]{:S(2)}) collective-permute-start(bf16[2,64,640]{2,1,0:T(8,128)(2,1)} %maximum_select_fusion), channel_id=1, source_target_pairs={{0,4},{28,24},{1,5},{29,25},{2,6},{30,26},{3,7},{31,27}} | collective-permute-start | bytes 491528 | tf_op jit(solution)/shard_map/ppermute | solution.py:588
  40.0 4.6 %all-to-all-start = ((bf16[48,64,384]{2,1,0:T(8,128)(2,1)}), bf16[48,64,384]{2,1,0:T(8,128)(2,1)S(1)}, u32[]{:S(2)}, u32[]{:S(2)}) async-start(bf16[48,64,384]{2,1,0:T(8,128)(2,1)} %gather.2), calls=%async_computation | async-start | bytes 4718592 | tf_op jit(solution)/shard_map/all_to_all | solution.py:614
  97.5 7.2 %collective-permute-done.4 = bf16[2,64,640]{2,1,0:T(8,128)(2,1)} collective-permute-done((bf16[2,64,640]{2,1,0:T(8,128)(2,1)}, bf16[2,64,640]{2,1,0:T(8,128)(2,1)}, u32[]{:S(2)}, u32[]{:S(2)}) %collective-permute-start.4) | collective-permute-done | bytes 163872 | tf_op jit(solution)/shard_map/ppermute | solution.py:594
  112.4 5.6 %collective-permute-done.5.b_ref = f32[2,64,256]{2,1,0:T(8,128)S(1)} collective-permute-done((f32[2,64,256]{2,1,0:T(8,128)S(1)}, f32[2,64,256]{2,1,0:T(8,128)S(1)}, u32[]{:S(2)}, u32[]{:S(2)}) %collective-permute-start.5) | collective-permute-done | bytes 131104 | tf_op jit(solution)/shard_map/ppermute | solution.py:604
  132.4 5.1 %collective-permute-done.7.b_ref = f32[2,64,256]{2,1,0:T(8,128)S(1)} collective-permute-done((f32[2,64,256]{2,1,0:T(8,128)}, f32[2,64,256]{2,1,0:T(8,128)S(1)}, u32[]{:S(2)}, u32[]{:S(2)}) %collective-permute-start.7) | collective-permute-done | bytes 131104 | tf_op jit(solution)/shard_map/ppermute | solution.py:609
  144.9 6.7 %sparse_fwd.2 = (bf16[512,256]{1,0:T(8,128)(2,1)}, f32[8,64,128]{2,1,0:T(8,128)}) custom-call(s32[48]{0:T(128)} %fusion.56.slot_ref, s32[3]{0:T(128)} %pad_add_fusion.meta_ref, bf16[8,64,256]{2,1,0:T(8,128)(2,1)} %bitcast.136, bf16[1,512,384]{2,1,0:T(8,128)(2,1)} %get-tuple-element.185.kv_ref, bf16[1,64,384]{2,1,0:T(8,128)(2,1)} %get-tuple-element.211.low_ref, ...), custom_call_target="tpu_custom_call" | custom-call | tf_op jit(solution)/shard_map/sparse_fwd/pallas_call | solution.py:31
  153.1 6.7 %sparse_fwd.3 = (bf16[512,256]{1,0:T(8,128)(2,1)}, f32[8,64,128]{2,1,0:T(8,128)}) custom-call(s32[48]{0:T(128)} %fusion.56.slot_ref, s32[3]{0:T(128)} %pad_add_fusion.meta_ref, bf16[8,64,256]{2,1,0:T(8,128)(2,1)} %bitcast.135, bf16[1,512,384]{2,1,0:T(8,128)(2,1)} %get-tuple-element.186.kv_ref, bf16[1,64,384]{2,1,0:T(8,128)(2,1)} %get-tuple-element.212.low_ref, ...), custom_call_target="tpu_custom_call" | custom-call | tf_op jit(solution)/shard_map/sparse_fwd/pallas_call | solution.py:31
  191.1 4.7 %all-to-all-start.1 = ((bf16[48,64,256]{2,1,0:T(8,128)(2,1)}), bf16[48,64,256]{2,1,0:T(8,128)(2,1)S(1)}, u32[]{:S(2)}, u32[]{:S(2)}) async-start(bf16[48,64,256]{2,1,0:T(8,128)(2,1)} %gather.3), calls=%async_computation.1 | async-start | bytes 3145728 | tf_op jit(solution)/shard_map/all_to_all | solution.py:614
  200.0 5.8 %ffn.2 = (bf16[512,768]{1,0:T(8,128)(2,1)}, bf16[512,768]{1,0:T(8,128)(2,1)}, bf16[512,768]{1,0:T(8,128)(2,1)}) custom-call(bf16[512,768]{1,0:T(8,128)(2,1)} %pad_maximum_fusion.1.act_ref, f32[512,768]{1,0:T(8,128)} %fusion.14.gu_ref, bf16[768,768]{1,0:T(8,128)(2,1)} %up_w_ref.3), custom_call_target="tpu_custom_call" | custom-call | tf_op jit(solution)/shard_map/ffn/pallas_call | solution.py:291
  207.9 5.9 %ffn.3 = (bf16[512,768]{1,0:T(8,128)(2,1)}, bf16[512,768]{1,0:T(8,128)(2,1)}, bf16[512,768]{1,0:T(8,128)(2,1)}) custom-call(bf16[512,768]{1,0:T(8,128)(2,1)} %pad_maximum_fusion.2.act_ref, f32[512,768]{1,0:T(8,128)} %fusion.22.gu_ref, bf16[768,768]{1,0:T(8,128)(2,1)} %up_w_ref.3), custom_call_target="tpu_custom_call" | custom-call | tf_op jit(solution)/shard_map/ffn/pallas_call | solution.py:291
  224.1 5.6 %collective-permute-done.21.got_ref = bf16[128,768]{1,0:T(8,128)(2,1)S(1)} collective-permute-done((bf16[128,768]{1,0:T(8,128)(2,1)S(1)}, bf16[128,768]{1,0:T(8,128)(2,1)S(1)}, u32[]{:S(2)}, u32[]{:S(2)}) %collective-permute-start.21) | collective-permute-done | bytes 196640 | tf_op jit(solution)/shard_map/ppermute | solution.py:566
  248.6 7.2 %heads_grad.1 = (bf16[16,64,256]{2,1,0:T(8,128)(2,1)}, bf16[48,64,256]{2,1,0:T(8,128)(2,1)}, bf16[2,64,256]{2,1,0:T(8,128)(2,1)}) custom-call(s32[48]{0:T(128)} %select_reduce_fusion.index_ref, s32[3]{0:T(128)} %pad_add_fusion.meta_ref, bf16[512,256]{1,0:T(8,128)(2,1)} %convolution_convert_fusion.6.refs_0_, ...), custom_call_target="tpu_custom_call" | custom-call | tf_op jit(solution)/shard_map/heads_grad/pallas_call | solution.py:31
  261.6 4.5 %all-to-all-start.2 = ((bf16[48,64,256]{2,1,0:T(8,128)(2,1)}), bf16[48,64,256]{2,1,0:T(8,128)(2,1)}, u32[]{:S(2)}, u32[]{:S(2)}) async-start(bf16[48,64,256]{2,1,0:T(8,128)(2,1)} %get-tuple-element.74), calls=%async_computation.2 | async-start | bytes 3145728 | tf_op jit(solution)/shard_map/all_to_all | solution.py:614
  273.3 4.5 %copy.157 = bf16[768,1728]{1,0:T(8,128)(2,1)} copy(bf16[768,1728]{0,1:T(8,128)(2,1)} %pad_maximum_fusion) | data formatting | bytes 5308416
  277.9 21.4 %collective-permute-done.29 = bf16[2,64,256]{2,1,0:T(8,128)(2,1)S(1)} collective-permute-done((bf16[2,64,256]{2,1,0:T(8,128)(2,1)S(1)}, bf16[2,64,256]{2,1,0:T(8,128)(2,1)S(1)}, u32[]{:S(2)}, u32[]{:S(2)}) %collective-permute-start.29) | collective-permute-done | bytes 65568 | tf_op jit(solution)/shard_map/ppermute | solution.py:588
  299.2 5.4 %collective-permute-start.30 = (bf16[2,64,256]{2,1,0:T(8,128)(2,1)S(1)}, bf16[2,64,256]{2,1,0:T(8,128)(2,1)S(1)}, u32[]{:S(2)}, u32[]{:S(2)}) collective-permute-start(bf16[2,64,256]{2,1,0:T(8,128)(2,1)S(1)} %broadcast_select_fusion.6), channel_id=1, source_target_pairs={{0,16},{4,20},{8,24},{12,28},{16,0},{20,4},{24,8},{28,12},{1,17},{... | collective-permute-start | bytes 196616 | tf_op jit(solution)/shard_map/ppermute | solution.py:594
  305.2 12.9 %sparse_bwd.1 = (f32[16,64,256]{2,1,0:T(8,128)}, f32[2,512,384]{2,1,0:T(8,128)}, bf16[2,64,384]{2,1,0:T(8,128)(2,1)}, bf16[2,64,384]{2,1,0:T(8,128)(2,1)}, f32[2,64,384]{2,1,0:T(8,128)}, /*index=5*/f32[2,64,384]{2,1,0:T(8,128)}) custom-call(s32[48]{0:T(128)} %fusion.56.slot_ref, bf16[16,64,256]{2,1,0:T(8,128)(2,1)} %bitcast.126, ...), custom_call_target="tpu_custom_call" | custom-call | tf_op jit(solution)/shard_map/sparse_bwd/pallas_call | solution.py:31
  320.1 6.8 %collective-permute-done.30 = bf16[2,64,256]{2,1,0:T(8,128)(2,1)S(1)} collective-permute-done((bf16[2,64,256]{2,1,0:T(8,128)(2,1)S(1)}, bf16[2,64,256]{2,1,0:T(8,128)(2,1)S(1)}, u32[]{:S(2)}, u32[]{:S(2)}) %collective-permute-start.30) | collective-permute-done | bytes 65568 | tf_op jit(solution)/shard_map/ppermute | solution.py:594
  334.1 5.6 %collective-permute-done.33 = bf16[2,64,640]{2,1,0:T(8,128)(2,1)S(1)} collective-permute-done((bf16[2,64,640]{2,1,0:T(8,128)(2,1)S(1)}, bf16[2,64,640]{2,1,0:T(8,128)(2,1)S(1)}, u32[]{:S(2)}, u32[]{:S(2)}) %collective-permute-start.33) | collective-permute-done | bytes 163872 | tf_op jit(solution)/shard_map/ppermute | solution.py:604
  350.4 4.6 %collective-permute-start.31 = (bf16[2,64,384]{2,1,0:T(8,128)(2,1)S(1)}, bf16[2,64,384]{2,1,0:T(8,128)(2,1)S(1)}, u32[]{:S(2)}, u32[]{:S(2)}) collective-permute-start(bf16[2,64,384]{2,1,0:T(8,128)(2,1)S(1)} %copy-done.69), channel_id=1, source_target_pairs={{0,4},{4,8},{8,12},{12,16},{16,20},{20,24},{24,28},{1,5},{5,9},{9,... | collective-permute-start | bytes 294920 | tf_op jit(solution)/shard_map/ppermute | solution.py:849
  362.8 26.7 %tail.1 = (bf16[768,640]{1,0:T(8,128)(2,1)}, bf16[2,512,768]{2,1,0:T(8,128)(2,1)}, f32[2,768]{1,0:T(2,128)}) custom-call(s32[48]{0:T(128)} %reshape.376.index_ref, s32[48]{0:T(128)} %reshape.395.valid_ref, s32[3]{0:T(128)} %pad_add_fusion.meta_ref, bf16[48,64,256]{2,1,0:T(8,128)(2,1)} %copy-done.3, bf16[48,64,256]{2,1,0:T(8,128)(2,1)} %all-to-all-done.2.do_got_ref, ...), custom_call_target="tpu_custom_call" | custom-call | tf_op jit(solution)/shard_map/tail/pallas_call | solution.py:31
  391.0 6.3 %all-to-all-start.4 = ((f32[32,4,96]{2,1,0:T(4,128)}), f32[32,4,96]{2,1,0:T(4,128)S(1)}, u32[]{:S(2)}, u32[]{:S(2)}) async-start(f32[32,4,96]{2,1,0:T(4,128)} %bitcast.53), calls=%async_computation.4 | async-start | bytes 131072 | tf_op jit(solution)/shard_map/all_to_all | solution.py:900
  (417 shorter events, 251.3 us)
Async XLA Ops:
  19.4 91.6 %collective-permute-start.1 = (bf16[2,64,384]{2,1,0:T(8,128)(2,1)}, bf16[2,64,384]{2,1,0:T(8,128)(2,1)}, u32[]{:S(2)}, u32[]{:S(2)}) collective-permute-start(bf16[2,64,384]{2,1,0:T(8,128)(2,1)} %get-tuple-element.187), channel_id=1, source_target_pairs={{4,0},{8,4},{12,8},{16,12},{20,16},{24,20},{28,24},{5,1},{9,5},{13... | collective-permute-start | bytes 294920 | tf_op jit(solution)/shard_map/ppermute | solution.py:702
  20.7 101.3 %collective-permute-start = (bf16[2,64,384]{2,1,0:T(8,128)(2,1)}, bf16[2,64,384]{2,1,0:T(8,128)(2,1)}, u32[]{:S(2)}, u32[]{:S(2)}) collective-permute-start(bf16[2,64,384]{2,1,0:T(8,128)(2,1)} %get-tuple-element.188), channel_id=1, source_target_pairs={{0,4},{4,8},{8,12},{12,16},{16,20},{20,24},{24,28},{1,5},{5,9},{9,... | collective-permute-start | bytes 294920 | tf_op jit(solution)/shard_map/ppermute | solution.py:701
  29.3 47.6 %collective-permute-start.2 = (bf16[2,64,640]{2,1,0:T(8,128)(2,1)}, bf16[2,64,640]{2,1,0:T(8,128)(2,1)}, u32[]{:S(2)}, u32[]{:S(2)}) collective-permute-start(bf16[2,64,640]{2,1,0:T(8,128)(2,1)} %maximum_select_fusion), channel_id=1, source_target_pairs={{0,4},{28,24},{1,5},{29,25},{2,6},{30,26},{3,7},{31,27}} | collective-permute-start | bytes 491528 | tf_op jit(solution)/shard_map/ppermute | solution.py:588
  40.0 103.4 %all-to-all-start = ((bf16[48,64,384]{2,1,0:T(8,128)(2,1)}), bf16[48,64,384]{2,1,0:T(8,128)(2,1)S(1)}, u32[]{:S(2)}, u32[]{:S(2)}) async-start(bf16[48,64,384]{2,1,0:T(8,128)(2,1)} %gather.2), calls=%async_computation | async-start | bytes 4718592 | tf_op jit(solution)/shard_map/all_to_all | solution.py:614
  86.4 18.3 %collective-permute-start.4 = (bf16[2,64,640]{2,1,0:T(8,128)(2,1)}, bf16[2,64,640]{2,1,0:T(8,128)(2,1)}, u32[]{:S(2)}, u32[]{:S(2)}) collective-permute-start(bf16[2,64,640]{2,1,0:T(8,128)(2,1)} %broadcast_select_fusion.1), channel_id=1, source_target_pairs={{0,16},{4,20},{8,24},{12,28},{16,0},{20,4},{24,8},{28,12},{1,17},{... | collective-permute-start | bytes 491528 | tf_op jit(solution)/shard_map/ppermute | solution.py:594
  153.1 16.7 %collective-permute-start.8 = (bf16[256,768]{1,0:T(8,128)(2,1)S(1)}, bf16[256,768]{1,0:T(8,128)(2,1)}, u32[]{:S(2)}, u32[]{:S(2)}) collective-permute-start(bf16[256,768]{1,0:T(8,128)(2,1)S(1)} %slice.389), channel_id=1, source_target_pairs={{0,1},{1,0},{2,3},{3,2},{4,5},{5,4},{6,7},{7,6},{8,9},{9,8},{10,11... | collective-permute-start | bytes 1179656 | tf_op jit(solution)/shard_map/ppermute | solution.py:566
  161.4 11.1 %collective-permute-start.14 = (bf16[256,768]{1,0:T(8,128)(2,1)S(1)}, bf16[256,768]{1,0:T(8,128)(2,1)}, u32[]{:S(2)}, u32[]{:S(2)}) collective-permute-start(bf16[256,768]{1,0:T(8,128)(2,1)S(1)} %slice.402), channel_id=1, source_target_pairs={{0,1},{1,0},{2,3},{3,2},{4,5},{5,4},{6,7},{7,6},{8,9},{9,8},{10,11... | collective-permute-start | bytes 1179656 | tf_op jit(solution)/shard_map/ppermute | solution.py:566
  173.6 10.2 %collective-permute-start.15 = (bf16[128,768]{1,0:T(8,128)(2,1)S(1)}, bf16[128,768]{1,0:T(8,128)(2,1)S(1)}, u32[]{:S(2)}, u32[]{:S(2)}) collective-permute-start(bf16[128,768]{1,0:T(8,128)(2,1)S(1)} %slice.471), channel_id=1, source_target_pairs={{0,2},{1,3},{2,0},{3,1},{4,6},{5,7},{6,4},{7,5},{8,10},{9,11},{10,... | collective-permute-start | bytes 589832 | tf_op jit(solution)/shard_map/ppermute | solution.py:566
  181.5 14.4 %collective-permute-start.10 = (bf16[128,768]{1,0:T(8,128)(2,1)}, bf16[128,768]{1,0:T(8,128)(2,1)S(1)}, u32[]{:S(2)}, u32[]{:S(2)}) collective-permute-start(bf16[128,768]{1,0:T(8,128)(2,1)} %get-tuple-element.60), channel_id=1, source_target_pairs={{0,2},{1,3},{2,0},{3,1},{4,6},{5,7},{6,4},{7,5},{8,10},{9,11},{10,... | collective-permute-start | bytes 589832 | tf_op jit(solution)/shard_map/ppermute | solution.py:566
  191.1 69.3 %all-to-all-start.1 = ((bf16[48,64,256]{2,1,0:T(8,128)(2,1)}), bf16[48,64,256]{2,1,0:T(8,128)(2,1)S(1)}, u32[]{:S(2)}, u32[]{:S(2)}) async-start(bf16[48,64,256]{2,1,0:T(8,128)(2,1)} %gather.3), calls=%async_computation.1 | async-start | bytes 3145728 | tf_op jit(solution)/shard_map/all_to_all | solution.py:614
  196.0 10.9 %collective-permute-start.17 = (bf16[256,768]{1,0:T(8,128)(2,1)S(1)}, bf16[256,768]{1,0:T(8,128)(2,1)S(1)}, u32[]{:S(2)}, u32[]{:S(2)}) collective-permute-start(bf16[256,768]{1,0:T(8,128)(2,1)S(1)} %pad_maximum_fusion.8), channel_id=1, source_target_pairs={{0,1},{1,0},{2,3},{3,2},{4,5},{5,4},{6,7},{7,6},{8,9},{9,8},{10,11... | collective-permute-start | bytes 1179656 | tf_op jit(solution)/shard_map/ppermute | solution.py:566
  206.9 14.1 %collective-permute-start.20 = (bf16[256,768]{1,0:T(8,128)(2,1)S(1)}, bf16[256,768]{1,0:T(8,128)(2,1)S(1)}, u32[]{:S(2)}, u32[]{:S(2)}) collective-permute-start(bf16[256,768]{1,0:T(8,128)(2,1)S(1)} %slice.342), channel_id=1, source_target_pairs={{0,1},{1,0},{2,3},{3,2},{4,5},{5,4},{6,7},{7,6},{8,9},{9,8},{10,11... | collective-permute-start | bytes 1179656 | tf_op jit(solution)/shard_map/ppermute | solution.py:566
  223.5 13.1 %collective-permute-start.25 = (bf16[128,768]{1,0:T(8,128)(2,1)S(1)}, bf16[128,768]{1,0:T(8,128)(2,1)S(1)}, u32[]{:S(2)}, u32[]{:S(2)}) collective-permute-start(bf16[128,768]{1,0:T(8,128)(2,1)S(1)} %slice.468), channel_id=1, source_target_pairs={{0,2},{1,3},{2,0},{3,1},{4,6},{5,7},{6,4},{7,5},{8,10},{9,11},{10,... | collective-permute-start | bytes 589832 | tf_op jit(solution)/shard_map/ppermute | solution.py:566
  255.8 10.4 %collective-permute-start.28 = (bf16[2,64,256]{2,1,0:T(8,128)(2,1)}, bf16[2,64,256]{2,1,0:T(8,128)(2,1)S(1)}, u32[]{:S(2)}, u32[]{:S(2)}) collective-permute-start(bf16[2,64,256]{2,1,0:T(8,128)(2,1)} %get-tuple-element.78), channel_id=1, source_target_pairs={{0,4},{28,24},{1,5},{29,25},{2,6},{30,26},{3,7},{31,27}} | collective-permute-start | bytes 196616 | tf_op jit(solution)/shard_map/ppermute | solution.py:588
  261.6 100.2 %all-to-all-start.2 = ((bf16[48,64,256]{2,1,0:T(8,128)(2,1)}), bf16[48,64,256]{2,1,0:T(8,128)(2,1)}, u32[]{:S(2)}, u32[]{:S(2)}) async-start(bf16[48,64,256]{2,1,0:T(8,128)(2,1)} %get-tuple-element.74), calls=%async_computation.2 | async-start | bytes 3145728 | tf_op jit(solution)/shard_map/all_to_all | solution.py:614
  266.1 169.9 %reduce-scatter.4.cloned.1.call-start = ((), (), s32[]{:S(2)}) async-start(), calls=%async_computation.6 | async-start | bytes 3096576
  266.2 33.0 %collective-permute-start.29 = (bf16[2,64,256]{2,1,0:T(8,128)(2,1)S(1)}, bf16[2,64,256]{2,1,0:T(8,128)(2,1)S(1)}, u32[]{:S(2)}, u32[]{:S(2)}) collective-permute-start(bf16[2,64,256]{2,1,0:T(8,128)(2,1)S(1)} %broadcast_select_fusion.5), channel_id=1, source_target_pairs={{0,8},{4,12},{28,20},{24,16},{1,9},{5,13},{29,21},{25,17},{2,10},{... | collective-permute-start | bytes 196616 | tf_op jit(solution)/shard_map/ppermute | solution.py:588
  299.2 27.6 %collective-permute-start.30 = (bf16[2,64,256]{2,1,0:T(8,128)(2,1)S(1)}, bf16[2,64,256]{2,1,0:T(8,128)(2,1)S(1)}, u32[]{:S(2)}, u32[]{:S(2)}) collective-permute-start(bf16[2,64,256]{2,1,0:T(8,128)(2,1)S(1)} %broadcast_select_fusion.6), channel_id=1, source_target_pairs={{0,16},{4,20},{8,24},{12,28},{16,0},{20,4},{24,8},{28,12},{1,17},{... | collective-permute-start | bytes 196616 | tf_op jit(solution)/shard_map/ppermute | solution.py:594
  343.1 54.1 %collective-permute-start.12 = (bf16[256,768]{1,0:T(8,128)(2,1)S(1)}, bf16[256,768]{1,0:T(8,128)(2,1)}, u32[]{:S(2)}, u32[]{:S(2)}) collective-permute-start(bf16[256,768]{1,0:T(8,128)(2,1)S(1)} %slice.393), channel_id=1, source_target_pairs={{0,1},{1,0},{2,3},{3,2},{4,5},{5,4},{6,7},{7,6},{8,9},{9,8},{10,11... | collective-permute-start | bytes 1179656 | tf_op jit(solution)/shard_map/ppermute | solution.py:566
  350.3 58.0 %collective-permute-start.18 = (bf16[256,768]{1,0:T(8,128)(2,1)S(1)}, bf16[256,768]{1,0:T(8,128)(2,1)}, u32[]{:S(2)}, u32[]{:S(2)}) collective-permute-start(bf16[256,768]{1,0:T(8,128)(2,1)S(1)} %slice.406), channel_id=1, source_target_pairs={{0,1},{1,0},{2,3},{3,2},{4,5},{5,4},{6,7},{7,6},{8,9},{9,8},{10,11... | collective-permute-start | bytes 1179656 | tf_op jit(solution)/shard_map/ppermute | solution.py:566
  391.0 13.8 %all-to-all-start.4 = ((f32[32,4,96]{2,1,0:T(4,128)}), f32[32,4,96]{2,1,0:T(4,128)S(1)}, u32[]{:S(2)}, u32[]{:S(2)}) async-start(f32[32,4,96]{2,1,0:T(4,128)} %bitcast.53), calls=%async_computation.4 | async-start | bytes 131072 | tf_op jit(solution)/shard_map/all_to_all | solution.py:900
  399.0 12.5 %collective-permute-start.13 = (bf16[128,768]{1,0:T(8,128)(2,1)}, bf16[128,768]{1,0:T(8,128)(2,1)}, u32[]{:S(2)}, u32[]{:S(2)}) collective-permute-start(bf16[128,768]{1,0:T(8,128)(2,1)} %slice.472), channel_id=1, source_target_pairs={{0,2},{1,3},{2,0},{3,1},{4,6},{5,7},{6,4},{7,5},{8,10},{9,11},{10,... | collective-permute-start | bytes 589832 | tf_op jit(solution)/shard_map/ppermute | solution.py:566
  404.8 30.3 %all-to-all-start.3 = ((bf16[8,96,640]{2,1,0:T(8,128)(2,1)}), bf16[8,96,640]{2,1,0:T(8,128)(2,1)S(1)}, u32[]{:S(2)}, u32[]{:S(2)}) async-start(bf16[8,96,640]{2,1,0:T(8,128)(2,1)} %bitcast.137), calls=%async_computation.3 | async-start | bytes 1966080 | tf_op jit(solution)/shard_map/all_to_all | solution.py:614
  419.6 10.4 %collective-permute-start.37 = (bf16[128,768]{1,0:T(8,128)(2,1)S(1)}, bf16[128,768]{1,0:T(8,128)(2,1)S(1)}, u32[]{:S(2)}, u32[]{:S(2)}) collective-permute-start(bf16[128,768]{1,0:T(8,128)(2,1)S(1)} %slice.467), channel_id=1, source_target_pairs={{0,2},{1,3},{2,0},{3,1},{4,6},{5,7},{6,4},{7,5},{8,10},{9,11},{10,... | collective-permute-start | bytes 589832 | tf_op jit(solution)/shard_map/ppermute | solution.py:566
  (94 other events, 605.0 us)
Sparse Core Ops, SparseCore 0:
  278.0 88.9 reduce-scatter.3
